TPU v7x, 32 devices: a whole 2x2x4 slice. The times are simulated.
32 devices in a mesh: groups: 2 (over x), wide: 4 (over y, core), narrow: 4 (over z).
Axes of the slice: x: 2, y: 2, z: 4, core: 2. Of those that a mesh axis runs over, the one named last changes fastest.
Arguments:
- coeffs: bfloat16 [16, 2, 512, 1536], P(('groups', 'wide'), None, 'narrow'), parts along dimension 0, may hold values from -0.109375 to 0.109375
- energies: bfloat16 [16, 512], P(('groups', 'wide'), 'narrow'), parts along dimension 0, may hold values from 1.59375 to 2.59375
- g_coupling: bfloat16 [16, 64, 936], P(('groups', 'narrow')), parts along dimension 0, may hold values from -0.75 to 0.75
- omega: float32 [16, 9], P('groups'), parts along dimension 0, may hold values from 0.02 to 0.2
- pairs: int32 [32, 2], P(('groups', 'wide')), parts along dimension 0, may hold values from 0 to 7, as said below
- counts: int32 [8], P('groups'), parts along dimension 0, may hold values from 1 to 4, 8 in all
- blocks: int32 [16, 512], P(('groups', 'wide')), parts along dimension 0, may hold values from 0 to 511, as said below
Outputs:
- linewidth: float32 [16, 512], P(('groups', 'wide'), 'narrow'), parts along dimension 0
There are 2 independent parts, one for each index of `groups`. A program takes and returns all parts, laid end to end along the dimension named above; each array names one. Nothing has to cross between parts.
Inputs may be any that keep to these rules, and one draw needn't show every extreme that they name: Worker w's rows are w * 4 to (w + 1) * 4 - 1; its live pairs are its first counts[w] rows. Each row's Q lies in w * 2 to (w + 1) * 2 - 1. Among one worker's 4 rows the owner ((Q + q) mod 8) // 2 takes any value at most 1 times, and some value exactly 1 times. Each exciton's label is the index of the first exciton of its degenerate block; blocks are 1 to 4 consecutive excitons, and some block holds exactly 4.
All inputs are finite; a program needn't handle non-finite values.
Results may differ from a plain program's by a relative error of at most 0.0003.
Values may be sent and summed in bfloat16 or wider, within the bound.
A program may use at most 192 MiB of HBM per device.

v0:
```python
import jax
import jax.numpy as jnp
from jax import lax
from jax.sharding import PartitionSpec as P

MODES = 9
CBANDS = 6
VBANDS = 4


broadening = 0.1


def padded(block, sides, width):
    for axis, dim in sides:
        count = lax.axis_size(axis)
        forward = [(i, i + 1) for i in range(count - 1)]
        backward = [(target, source) for source, target in forward]
        low = lax.ppermute(
            lax.slice_in_dim(block, block.shape[dim] - width, None, axis=dim), axis, forward
        )
        high = lax.ppermute(lax.slice_in_dim(block, 0, width, axis=dim), axis, backward)
        block = jnp.concatenate([low, block, high], axis=dim)
    return block


def pick_rows(current, segment, wanted):
    row_count = segment.shape[0]
    inside = (wanted >= 0) & (wanted < row_count)
    chosen = jnp.take(segment, jnp.clip(wanted, 0, row_count - 1), axis=0)
    keep_row = inside.reshape((-1,) + (1,) * (chosen.ndim - 1))
    return jnp.where(keep_row, chosen, current)


def pair_rate(own_rows, own_levels, far_rows, far_levels, coupling_row, shift_index, phonons):
    momenta = phonons.shape[0]
    kpoints = coupling_row.shape[0]
    columns = own_rows.shape[1]
    cut_point = 2 * MODES * CBANDS * CBANDS
    electron = coupling_row[:, :cut_point].reshape(kpoints, 2, MODES, CBANDS, CBANDS)
    hole_part = coupling_row[:, cut_point:].reshape(kpoints, 2, MODES, VBANDS, VBANDS)
    real_rows = own_rows[0].reshape(columns, kpoints, CBANDS, VBANDS)
    imag_rows = own_rows[1].reshape(columns, kpoints, CBANDS, VBANDS)

    def by_electron(gain, rows):
        return jnp.einsum("kucd,nkdv->unkcv", gain, rows, preferred_element_type=jnp.float32)

    def by_hole(gain, rows):
        return jnp.einsum("kuvw,nkcw->unkcv", gain, rows, preferred_element_type=jnp.float32)

    elec_real, elec_imag = (electron[:, 0], electron[:, 1])
    hole_real, hole_imag = (hole_part[:, 0], hole_part[:, 1])
    real_out = (
        by_electron(elec_real, real_rows)
        - by_electron(elec_imag, imag_rows)
        - by_hole(hole_real, real_rows)
        + by_hole(hole_imag, imag_rows)
    )
    imag_out = (
        by_electron(elec_real, imag_rows)
        + by_electron(elec_imag, real_rows)
        - by_hole(hole_real, imag_rows)
        - by_hole(hole_imag, real_rows)
    )
    real_mix = real_out.astype(jnp.bfloat16).reshape(MODES, columns, -1)
    imag_mix = imag_out.astype(jnp.bfloat16).reshape(MODES, columns, -1)
    left_side = jnp.concatenate([far_rows[0], far_rows[1]], axis=-1)
    upper = jnp.concatenate([real_mix, imag_mix], axis=-1)
    lower = jnp.concatenate([imag_mix, -real_mix], axis=-1)
    right_side = jnp.concatenate([upper, lower], axis=0).reshape(
        2 * MODES * columns, left_side.shape[1]
    )
    coupled = lax.dot_general(
        left_side, right_side, (((1,), (1,)), ((), ())), preferred_element_type=jnp.float32
    )
    coupled = coupled.reshape(left_side.shape[0], 2, MODES, columns)
    power = coupled[:, 0] * coupled[:, 0] + coupled[:, 1] * coupled[:, 1]
    frequency = jnp.sum(
        jnp.where(jnp.arange(momenta)[:, None] == shift_index, phonons, 0.0), axis=0
    )
    detuning = (
        far_levels.astype(jnp.float32)[:, None, None]
        - own_levels.astype(jnp.float32)[None, None, :]
        - frequency[None, :, None]
    )
    weight = 1.0 / (1.0 + (detuning / broadening) ** 2)
    return jnp.sum(power * weight, axis=(0, 1))


def shards(coeffs, energies, g_coupling, omega, pairs, counts, blocks):
    worker = lax.axis_index("wide")
    workers = lax.axis_size("wide")
    owned = coeffs.shape[0]
    columns = coeffs.shape[2]
    momenta = owned * workers
    slots = pairs.shape[0]
    home_index = pairs[:, 0]
    shift_index = pairs[:, 1]
    far_index = (home_index + shift_index) % momenta
    local_index = home_index - worker * owned
    own_a = jnp.take(coeffs, local_index, axis=0)
    own_e = jnp.take(energies, local_index, axis=0)
    active = (jnp.arange(slots) < jnp.take(counts, worker)).astype(jnp.float32)
    far_a = pick_rows(
        jnp.zeros((slots,) + coeffs.shape[1:], coeffs.dtype),
        lax.all_gather(coeffs, "wide", axis=0, tiled=True),
        far_index,
    )
    far_e = pick_rows(
        jnp.zeros((slots, columns), energies.dtype),
        lax.all_gather(energies, "wide", axis=0, tiled=True),
        far_index,
    )
    far_a, far_e = (
        lax.all_gather(far_a, "narrow", axis=2, tiled=True),
        lax.all_gather(far_e, "narrow", axis=1, tiled=True),
    )
    blank_g = jnp.zeros((shift_index.shape[0],) + g_coupling.shape[1:], g_coupling.dtype)
    coupling_rows = pick_rows(
        blank_g, lax.all_gather(g_coupling, "narrow", axis=0, tiled=True), shift_index
    )

    def one_slot(items):
        return pair_rate(items[0], items[1], items[2], items[3], items[4], items[5], omega)

    rates = lax.map(one_slot, (own_a, own_e, far_a, far_e, coupling_rows, shift_index))
    rates = rates * active[:, None]
    onehot = ((home_index - worker * owned)[:, None] == jnp.arange(owned)[None, :]).astype(
        jnp.float32
    )
    home_rates = jnp.dot(onehot.T, rates, precision=lax.Precision.HIGHEST)
    margin = 3
    widened = padded(home_rates, (("narrow", 1),), margin)
    part_index = lax.axis_index("narrow")
    padded_labels = jnp.pad(blocks, ((0, 0), (margin, margin)), constant_values=-1)
    near_labels = lax.dynamic_slice_in_dim(
        padded_labels, part_index * columns, columns + 2 * margin, 1
    )
    my_labels = lax.dynamic_slice_in_dim(blocks, part_index * columns, columns, 1)
    same = (my_labels[:, :, None] == near_labels[:, None, :]).astype(jnp.float32)
    return jnp.sum(same * widened[:, None, :], axis=2) / jnp.sum(same, axis=2)


def solution(mesh):
    in_specs = (
        P(("groups", "wide"), None, "narrow", None),
        P(("groups", "wide"), "narrow"),
        P(("groups", "narrow"), None, None),
        P("groups", None),
        P(("groups", "wide"), None),
        P("groups"),
        P(("groups", "wide"), None),
    )
    out_specs = P(("groups", "wide"), "narrow")
    return jax.shard_map(shards, mesh=mesh, in_specs=in_specs, out_specs=out_specs, check_vma=False)
```

profile of v0, /device:TPU:0, one launch (start us, length us, event | category | flops | bytes accessed | tf_op | source)
XLA Modules:
  0.0 935.0 jit_solution(16711741815974156283)
XLA Ops:
  8.9 49.1 %all-gather.4.cloned.1.call-done = bf16[8,2,128,1536]{3,2,1,0:T(8,128)(2,1)} async-done(((bf16[2,2,128,1536]{3,2,1,0:T(8,128)(2,1)}), bf16[8,2,128,1536]{3,2,1,0:T(8,128)(2,1)}) %all-gather.4.cloned.1.call-update) | async-done | bytes 6291472 | tf_op jit(solution)/shard_map/all_gather | solution.py:106
  58.0 5.2 gather_fusion
  63.2 4.1 select_select_fusion
  67.4 2.4 gather_fusion.1
  70.3 5.2 all-gather
  78.1 41.2 %all_gather.17 = bf16[8,64,936]{2,1,0:T(8,128)(2,1)} all-gather(bf16[2,64,936]{2,1,0:T(8,128)(2,1)S(1)} %copy-done.13), channel_id=1, replica_groups=mesh['groups'=2,'wide'=4,'narrow'=4] {'narrow'}, dimensions={0}, use_global_device_ids=true | all-gather | bytes 1198080 | tf_op jit(solution)/shard_map/all_gather | solution.py:120
  119.3 2.6 gather_fusion.2
  122.6 12.5 %all_gather.19 = bf16[4,512]{1,0:T(4,128)(2,1)S(1)} all-gather(bf16[4,128]{1,0:T(4,128)(2,1)S(1)} %select_select_fusion.2), channel_id=1, replica_groups=mesh['groups'=2,'wide'=4,'narrow'=4] {'narrow'}, dimensions={1}, use_global_device_ids=true | all-gather | bytes 5120 | tf_op jit(solution)/shard_map/all_gather | solution.py:116
  138.3 2.0 broadcast_select_fusion
  140.3 162.2 %all-gather.6.cloned.1.call-done = bf16[4,2,512,1536]{3,2,1,0:T(8,128)(2,1)} async-done(((bf16[4,2,128,1536]{3,2,1,0:T(8,128)(2,1)}), bf16[4,2,512,1536]{3,2,1,0:T(8,128)(2,1)}) %all-gather.6.cloned.1.call-update) | async-done | bytes 12582928 | tf_op jit(solution)/shard_map/all_gather | solution.py:115
  302.5 615.5 %while.11 = (s32[]{:T(128)}, f32[4,128]{1,0:T(4,128)}, bf16[4,2,512,1536]{3,2,1,0:T(8,128)(2,1)}, bf16[4,2,128,1536]{3,2,1,0:T(8,128)(2,1)}, bf16[4,64,936]{2,1,...) while((s32[]{:T(128)}, f32[4,128]{1,0:T(4,128)}, ...), condition=%wide.region_3.4_spmd, body=%wide.region_0.3_spmd.sunk | while | flops 7474119168 | bytes 186653376 | solution.py:126
  328.9 6.4 fusion.102
  336.3 6.5 fusion.103
  343.1 6.3 fusion.101
  350.5 15.9 %fusion.104 = bf16[9,128,64,6,4]{1,0,3,4,2:T(8,128)(2,1)} fusion(f32[64,128,6,9,4]{1,3,2,4,0:T(8,128)} %fusion.101, f32[64,128,4,9,6]{1,3,4,2,0:T(8,128)} %fusion.102, f32[64,128,4,9,6]{1,3,4,2,0:T(8,128)} %fusion.103, bf16[128,64,6,4,1]{0,3,2,4,1:T(4,128)(2,1)S(1)} %bitcast.212, bf16[64,1,9,4,4]{2,4,3,0,1:T(4,128)(2,1)S(1)} %copy.131), kind=kOutput, calls=%fused_computation.7.clone.1 | convolution fusion | flops 21233664 | bytes 25184256 | tf_op jit(solution)/shard_map/while/body/eval_jaxpr/kuvw,nkcw->unkcv/dot_general | solution.py:49
  366.3 4.8 copy.133
  371.2 6.4 fusion.98
  377.6 6.5 fusion.99
  384.0 6.3 fusion.96
  390.4 16.8 %fusion.100 = bf16[9,128,64,6,4]{1,0,3,4,2:T(8,128)(2,1)} fusion(f32[64,128,6,9,4]{1,3,2,4,0:T(8,128)} %fusion.96, f32[64,128,4,9,6]{1,3,4,2,0:T(8,128)} %fusion.98, f32[64,128,4,9,6]{1,3,4,2,0:T(8,128)} %fusion.99, bf16[128,64,6,4,1]{0,3,2,4,1:T(4,128)(2,1)} %bitcast.209, bf16[64,1,9,4,4]{2,4,3,0,1:T(4,128)(2,1)} %copy-done.8), kind=kOutput, calls=%fused_computation.10.clone.1 | convolution fusion | flops 21233664 | bytes 25184256 | tf_op jit(solution)/shard_map/while/body/eval_jaxpr/kuvw,nkcw->unkcv/dot_general | solution.py:49
  407.2 4.7 copy.132
  412.6 47.8 %maximum_maximum_fusion.2 = bf16[18,128,3072]{1,2,0:T(8,128)(2,1)S(1)} fusion(bf16[9,128,1536]{1,2,0:T(8,128)(2,1)S(1)} %neg.4, bf16[9,128,1536]{1,2,0:T(8,128)(2,1)S(1)} %bitcast.206, bf16[9,128,1536]{1,2,0:T(8,128)(2,1)S(1)} %bitcast.204), kind=kLoop, calls=%fused_computation.5.clone.1 | loop fusion | flops 56623104 | bytes 24772608 | tf_op jit(solution)/shard_map/while/body/eval_jaxpr/concatenate | solution.py:70
  460.4 2.1 dynamic-slice_bitcast_fusion.3
  462.6 7.5 fusion.105
  477.1 6.4 fusion.102
  484.4 6.5 fusion.103
  491.3 6.3 fusion.101
  498.6 15.9 %fusion.104 = bf16[9,128,64,6,4]{1,0,3,4,2:T(8,128)(2,1)} fusion(f32[64,128,6,9,4]{1,3,2,4,0:T(8,128)} %fusion.101, f32[64,128,4,9,6]{1,3,4,2,0:T(8,128)} %fusion.102, f32[64,128,4,9,6]{1,3,4,2,0:T(8,128)} %fusion.103, bf16[128,64,6,4,1]{0,3,2,4,1:T(4,128)(2,1)S(1)} %bitcast.212, bf16[64,1,9,4,4]{2,4,3,0,1:T(4,128)(2,1)S(1)} %copy.131), kind=kOutput, calls=%fused_computation.7.clone.1 | convolution fusion | flops 21233664 | bytes 25184256 | tf_op jit(solution)/shard_map/while/body/eval_jaxpr/kuvw,nkcw->unkcv/dot_general | solution.py:49
  514.5 4.8 copy.133
  519.3 6.4 fusion.98
  525.7 6.5 fusion.99
  532.2 6.3 fusion.96
  538.5 16.8 %fusion.100 = bf16[9,128,64,6,4]{1,0,3,4,2:T(8,128)(2,1)} fusion(f32[64,128,6,9,4]{1,3,2,4,0:T(8,128)} %fusion.96, f32[64,128,4,9,6]{1,3,4,2,0:T(8,128)} %fusion.98, f32[64,128,4,9,6]{1,3,4,2,0:T(8,128)} %fusion.99, bf16[128,64,6,4,1]{0,3,2,4,1:T(4,128)(2,1)} %bitcast.209, bf16[64,1,9,4,4]{2,4,3,0,1:T(4,128)(2,1)} %copy-done.8), kind=kOutput, calls=%fused_computation.10.clone.1 | convolution fusion | flops 21233664 | bytes 25184256 | tf_op jit(solution)/shard_map/while/body/eval_jaxpr/kuvw,nkcw->unkcv/dot_general | solution.py:49
  555.3 4.7 copy.132
  560.8 47.8 %maximum_maximum_fusion.2 = bf16[18,128,3072]{1,2,0:T(8,128)(2,1)S(1)} fusion(bf16[9,128,1536]{1,2,0:T(8,128)(2,1)S(1)} %neg.4, bf16[9,128,1536]{1,2,0:T(8,128)(2,1)S(1)} %bitcast.206, bf16[9,128,1536]{1,2,0:T(8,128)(2,1)S(1)} %bitcast.204), kind=kLoop, calls=%fused_computation.5.clone.1 | loop fusion | flops 56623104 | bytes 24772608 | tf_op jit(solution)/shard_map/while/body/eval_jaxpr/concatenate | solution.py:70
  608.6 2.1 dynamic-slice_bitcast_fusion.3
  610.7 7.5 fusion.105
  625.3 6.4 fusion.102
  632.6 6.5 fusion.103
  639.4 6.3 fusion.101
  646.8 15.9 %fusion.104 = bf16[9,128,64,6,4]{1,0,3,4,2:T(8,128)(2,1)} fusion(f32[64,128,6,9,4]{1,3,2,4,0:T(8,128)} %fusion.101, f32[64,128,4,9,6]{1,3,4,2,0:T(8,128)} %fusion.102, f32[64,128,4,9,6]{1,3,4,2,0:T(8,128)} %fusion.103, bf16[128,64,6,4,1]{0,3,2,4,1:T(4,128)(2,1)S(1)} %bitcast.212, bf16[64,1,9,4,4]{2,4,3,0,1:T(4,128)(2,1)S(1)} %copy.131), kind=kOutput, calls=%fused_computation.7.clone.1 | convolution fusion | flops 21233664 | bytes 25184256 | tf_op jit(solution)/shard_map/while/body/eval_jaxpr/kuvw,nkcw->unkcv/dot_general | solution.py:49
  662.6 4.8 copy.133
  667.5 6.4 fusion.98
  673.9 6.5 fusion.99
  680.3 6.3 fusion.96
  686.7 16.8 %fusion.100 = bf16[9,128,64,6,4]{1,0,3,4,2:T(8,128)(2,1)} fusion(f32[64,128,6,9,4]{1,3,2,4,0:T(8,128)} %fusion.96, f32[64,128,4,9,6]{1,3,4,2,0:T(8,128)} %fusion.98, f32[64,128,4,9,6]{1,3,4,2,0:T(8,128)} %fusion.99, bf16[128,64,6,4,1]{0,3,2,4,1:T(4,128)(2,1)} %bitcast.209, bf16[64,1,9,4,4]{2,4,3,0,1:T(4,128)(2,1)} %copy-done.8), kind=kOutput, calls=%fused_computation.10.clone.1 | convolution fusion | flops 21233664 | bytes 25184256 | tf_op jit(solution)/shard_map/while/body/eval_jaxpr/kuvw,nkcw->unkcv/dot_general | solution.py:49
  703.4 4.7 copy.132
  708.9 47.8 %maximum_maximum_fusion.2 = bf16[18,128,3072]{1,2,0:T(8,128)(2,1)S(1)} fusion(bf16[9,128,1536]{1,2,0:T(8,128)(2,1)S(1)} %neg.4, bf16[9,128,1536]{1,2,0:T(8,128)(2,1)S(1)} %bitcast.206, bf16[9,128,1536]{1,2,0:T(8,128)(2,1)S(1)} %bitcast.204), kind=kLoop, calls=%fused_computation.5.clone.1 | loop fusion | flops 56623104 | bytes 24772608 | tf_op jit(solution)/shard_map/while/body/eval_jaxpr/concatenate | solution.py:70
  756.7 2.1 dynamic-slice_bitcast_fusion.3
  758.8 7.5 fusion.105
  773.4 6.4 fusion.102
  780.7 6.5 fusion.103
  787.5 6.3 fusion.101
  794.9 15.9 %fusion.104 = bf16[9,128,64,6,4]{1,0,3,4,2:T(8,128)(2,1)} fusion(f32[64,128,6,9,4]{1,3,2,4,0:T(8,128)} %fusion.101, f32[64,128,4,9,6]{1,3,4,2,0:T(8,128)} %fusion.102, f32[64,128,4,9,6]{1,3,4,2,0:T(8,128)} %fusion.103, bf16[128,64,6,4,1]{0,3,2,4,1:T(4,128)(2,1)S(1)} %bitcast.212, bf16[64,1,9,4,4]{2,4,3,0,1:T(4,128)(2,1)S(1)} %copy.131), kind=kOutput, calls=%fused_computation.7.clone.1 | convolution fusion | flops 21233664 | bytes 25184256 | tf_op jit(solution)/shard_map/while/body/eval_jaxpr/kuvw,nkcw->unkcv/dot_general | solution.py:49
  810.8 4.8 copy.133
  815.6 6.4 fusion.98
  822.0 6.5 fusion.99
  828.5 6.3 fusion.96
  834.8 16.8 %fusion.100 = bf16[9,128,64,6,4]{1,0,3,4,2:T(8,128)(2,1)} fusion(f32[64,128,6,9,4]{1,3,2,4,0:T(8,128)} %fusion.96, f32[64,128,4,9,6]{1,3,4,2,0:T(8,128)} %fusion.98, f32[64,128,4,9,6]{1,3,4,2,0:T(8,128)} %fusion.99, bf16[128,64,6,4,1]{0,3,2,4,1:T(4,128)(2,1)} %bitcast.209, bf16[64,1,9,4,4]{2,4,3,0,1:T(4,128)(2,1)} %copy-done.8), kind=kOutput, calls=%fused_computation.10.clone.1 | convolution fusion | flops 21233664 | bytes 25184256 | tf_op jit(solution)/shard_map/while/body/eval_jaxpr/kuvw,nkcw->unkcv/dot_general | solution.py:49
  851.6 4.7 copy.132
  857.1 47.8 %maximum_maximum_fusion.2 = bf16[18,128,3072]{1,2,0:T(8,128)(2,1)S(1)} fusion(bf16[9,128,1536]{1,2,0:T(8,128)(2,1)S(1)} %neg.4, bf16[9,128,1536]{1,2,0:T(8,128)(2,1)S(1)} %bitcast.206, bf16[9,128,1536]{1,2,0:T(8,128)(2,1)S(1)} %bitcast.204), kind=kLoop, calls=%fused_computation.5.clone.1 | loop fusion | flops 56623104 | bytes 24772608 | tf_op jit(solution)/shard_map/while/body/eval_jaxpr/concatenate | solution.py:70
  904.9 2.1 dynamic-slice_bitcast_fusion.3
  907.0 7.5 fusion.105
  921.6 4.2 collective-permute-done.1
  (238 shorter events, 54.4 us)
Async XLA Ops:
  6.5 51.5 %all-gather.4.cloned.1.call-start = ((), (), s32[]{:S(2)}) async-start(), calls=%async_computation | async-start | bytes 7864320 | tf_op jit(solution)/shard_map/all_gather | solution.py:106
  7.3 295.3 %all-gather.6.cloned.1.call-start = ((), (), s32[]{:S(2)}) async-start(), calls=%async_computation.1 | async-start | bytes 15728640 | tf_op jit(solution)/shard_map/all_gather | solution.py:115
  63.2 4.2 copy-start.11
  67.3 2.5 copy-start.14
  67.3 8.8 copy-start.20
  67.3 9.4 %copy-start.17 = (s32[2,512]{1,0:T(2,128)S(1)}, s32[2,512]{1,0:T(2,128)}, u32[]{:S(2)}) copy-start(s32[2,512]{1,0:T(2,128)} %param.15) | copy-start | bytes 12292
  67.3 10.2 %copy-start.16 = (s32[4,2]{0,1:T(2,128)S(1)}, s32[4,2]{0,1:T(2,128)}, u32[]{:S(2)}) copy-start(s32[4,2]{0,1:T(2,128)} %param.13) | copy-start | bytes 100
  67.3 10.8 %copy-start.13 = (bf16[2,64,936]{2,1,0:T(8,128)(2,1)S(1)}, bf16[2,64,936]{2,1,0:T(8,128)(2,1)}, u32[]{:S(2)}) copy-start(bf16[2,64,936]{2,1,0:T(8,128)(2,1)} %param.11) | copy-start | bytes 718852
  69.8 68.5 %copy-start.12 = (bf16[4,2,128,1536]{3,2,1,0:T(8,128)(2,1)S(1)}, bf16[4,2,128,1536]{3,2,1,0:T(8,128)(2,1)}, u32[]{:S(2)}) copy-start(bf16[4,2,128,1536]{3,2,1,0:T(8,128)(2,1)} %gather_fusion.1) | copy-start | bytes 9437188
  136.3 166.2 %copy-start.15 = (f32[8,9]{1,0:T(8,128)S(1)}, f32[8,9]{1,0:T(8,128)}, u32[]{:S(2)}) copy-start(f32[8,9]{1,0:T(8,128)} %param.12) | copy-start | bytes 868
  302.5 623.5 %copy-start.18 = (s32[2,128]{1,0:T(2,128)S(1)}, s32[2,128]{1,0:T(2,128)}, u32[]{:S(2)}) copy-start(s32[2,128]{1,0:T(2,128)} %constant_dynamic-slice_fusion.4) | copy-start | bytes 3076
  326.8 16.2 %copy-start = (bf16[1,1,128,1536]{2,3,1,0:T(8,128)(2,1)}, bf16[1,1,128,1536]{2,3,1,0:T(8,128)(2,1)S(1)}, u32[]{:S(2)}) copy-start(bf16[1,1,128,1536]{2,3,1,0:T(8,128)(2,1)S(1)} %copy.130) | copy-start | bytes 1179652 | tf_op jit(solution)/shard_map/while
  328.9 6.4 copy-start.4
  335.6 14.2 %copy-start.2 = (bf16[1,1,128,1536]{2,3,1,0:T(8,128)(2,1)}, bf16[1,1,128,1536]{2,3,1,0:T(8,128)(2,1)S(1)}, u32[]{:S(2)}) copy-start(bf16[1,1,128,1536]{2,3,1,0:T(8,128)(2,1)S(1)} %copy.125) | copy-start | bytes 1179652 | tf_op jit(solution)/shard_map/while
  336.3 6.5 copy-start.6
  343.1 6.4 copy-start.9
  349.8 0.7 copy-start.8
  366.3 4.8 copy-start.3
  366.3 4.8 copy-start.5
  371.2 6.4 copy-start.1
  371.2 6.4 copy-start.7
  377.6 6.5 copy-start.10
  462.5 7.6 copy-start.19
  475.0 16.2 %copy-start = (bf16[1,1,128,1536]{2,3,1,0:T(8,128)(2,1)}, bf16[1,1,128,1536]{2,3,1,0:T(8,128)(2,1)S(1)}, u32[]{:S(2)}) copy-start(bf16[1,1,128,1536]{2,3,1,0:T(8,128)(2,1)S(1)} %copy.130) | copy-start | bytes 1179652 | tf_op jit(solution)/shard_map/while
  477.1 6.4 copy-start.4
  483.7 14.2 %copy-start.2 = (bf16[1,1,128,1536]{2,3,1,0:T(8,128)(2,1)}, bf16[1,1,128,1536]{2,3,1,0:T(8,128)(2,1)S(1)}, u32[]{:S(2)}) copy-start(bf16[1,1,128,1536]{2,3,1,0:T(8,128)(2,1)S(1)} %copy.125) | copy-start | bytes 1179652 | tf_op jit(solution)/shard_map/while
  484.4 6.5 copy-start.6
  491.3 6.3 copy-start.9
  497.9 0.7 copy-start.8
  514.5 4.8 copy-start.3
  514.5 4.8 copy-start.5
  519.3 6.4 copy-start.1
  519.3 6.4 copy-start.7
  525.7 6.5 copy-start.10
  610.7 7.6 copy-start.19
  623.1 16.2 %copy-start = (bf16[1,1,128,1536]{2,3,1,0:T(8,128)(2,1)}, bf16[1,1,128,1536]{2,3,1,0:T(8,128)(2,1)S(1)}, u32[]{:S(2)}) copy-start(bf16[1,1,128,1536]{2,3,1,0:T(8,128)(2,1)S(1)} %copy.130) | copy-start | bytes 1179652 | tf_op jit(solution)/shard_map/while
  625.2 6.4 copy-start.4
  631.9 14.2 %copy-start.2 = (bf16[1,1,128,1536]{2,3,1,0:T(8,128)(2,1)}, bf16[1,1,128,1536]{2,3,1,0:T(8,128)(2,1)S(1)}, u32[]{:S(2)}) copy-start(bf16[1,1,128,1536]{2,3,1,0:T(8,128)(2,1)S(1)} %copy.125) | copy-start | bytes 1179652 | tf_op jit(solution)/shard_map/while
  632.6 6.5 copy-start.6
  639.4 6.3 copy-start.9
  646.1 0.7 copy-start.8
  662.6 4.8 copy-start.3
  662.6 4.8 copy-start.5
  667.5 6.4 copy-start.1
  667.5 6.4 copy-start.7
  673.9 6.5 copy-start.10
  758.8 7.6 copy-start.19
  771.3 16.2 %copy-start = (bf16[1,1,128,1536]{2,3,1,0:T(8,128)(2,1)}, bf16[1,1,128,1536]{2,3,1,0:T(8,128)(2,1)S(1)}, u32[]{:S(2)}) copy-start(bf16[1,1,128,1536]{2,3,1,0:T(8,128)(2,1)S(1)} %copy.130) | copy-start | bytes 1179652 | tf_op jit(solution)/shard_map/while
  773.4 6.4 copy-start.4
  780.0 14.2 %copy-start.2 = (bf16[1,1,128,1536]{2,3,1,0:T(8,128)(2,1)}, bf16[1,1,128,1536]{2,3,1,0:T(8,128)(2,1)S(1)}, u32[]{:S(2)}) copy-start(bf16[1,1,128,1536]{2,3,1,0:T(8,128)(2,1)S(1)} %copy.125) | copy-start | bytes 1179652 | tf_op jit(solution)/shard_map/while
  780.7 6.5 copy-start.6
  787.5 6.3 copy-start.9
  794.2 0.7 copy-start.8
  810.8 4.8 copy-start.3
  810.8 4.8 copy-start.5
  815.6 6.4 copy-start.1
  815.6 6.4 copy-start.7
  822.0 6.5 copy-start.10
  907.0 7.6 copy-start.19
  919.0 2.6 collective-permute-start
  920.3 5.5 collective-permute-start.1
Sparse Core Ops, SparseCore 0:
  8.9 49.0 all-gather.3
  67.4 235.0 all-gather.5
where the time goes:
time: 938 us; the launch traced here: 935 us
  matrix products  315 us (34%)
  waiting for transfers between devices  216 us (23%)
  other arithmetic  214 us (23%)
  local copies, waits for them, and re-layouts  90.2 us (10%)
  blocking collectives  58.8 us (6%)
  loops' own time  24 us (3%)
  between operations  14.6 us (2%)
    concatenate x4, other arithmetic, pair_rate(): jnp.concatenate([upper, lower], axis=0)  191 us
    dot_general x16, matrix products, by_hole(): jnp.einsum('kuvw,nkcw->unkcv', gain, rows, preferred_element_type=jnp.flo...  181 us
    all_gather x1, waiting for transfers between devices, shards(): lax.all_gather(far_a, 'narrow', axis=2, tiled=True)  162 us
    dot_general x16, matrix products, by_electron(): jnp.einsum('kucd,nkdv->unkcv', gain, rows, preferred_element_type=jnp.flo...  103 us
    all_gather x1, waiting for transfers between devices, shards(): lax.all_gather(coeffs, 'wide', axis=0, tiled=True)  49.1 us
    all_gather x1, blocking collectives, shards(): lax.all_gather(g_coupling, 'narrow', axis=0, tiled=True)  41.2 us
    dot_general x4, matrix products, pair_rate(): lax.dot_general(left_side, right_side, (((1,), (1,)), ((), ())), preferre...  29.8 us
    another operation x1, loops' own time, shards(): lax.map(one_slot, (own_a, own_e, far_a, far_e, coupling_rows, shift_index))  24 us
  transfers between devices with their start and end apart: 4, of which 3 were waited for; matrix products, arithmetic and copies ran while one was open for 2% of the time, Pallas kernels for 0%

commit v1 on v0

v1 whole, which is shorter than its diff:
```python
import functools

import jax
import jax.numpy as jnp
import numpy as np
from jax import lax
from jax.experimental import pallas as pl
from jax.experimental.pallas import tpu as pltpu
from jax.sharding import PartitionSpec as P

MODES = 9
CBANDS = 6
VBANDS = 4
BANDS = CBANDS * VBANDS
ROWS = MODES * 2 * BANDS

broadening = 0.1


def expansion_tables():
    u, pout, c, v = np.unravel_index(np.arange(ROWS), (MODES, 2, CBANDS, VBANDS))
    cut = 2 * MODES * CBANDS * CBANDS
    index, mask = [], []
    for pin in range(2):
        part = pout ^ pin
        sign = np.where((pout == 0) & (pin == 1), -1.0, 1.0)
        for d in range(CBANDS):
            index.append(((part * MODES + u) * CBANDS + c) * CBANDS + d)
            mask.append(np.stack([sign * (v == other) for other in range(VBANDS)]))
    electron_mask = np.stack(mask)
    mask = []
    for pin in range(2):
        part = pout ^ pin
        sign = np.where((pout == 0) & (pin == 1), 1.0, -1.0)
        for w in range(VBANDS):
            index.append(cut + ((part * MODES + u) * VBANDS + v) * VBANDS + w)
            mask.append(np.stack([sign * (c == other) for other in range(CBANDS)]))
    hole_mask = np.stack(mask)
    return np.stack(index).astype(np.int32), electron_mask, hole_mask


def expand_coupling(chosen):
    index, electron_mask, hole_mask = expansion_tables()
    share, kpoints, width = chosen.shape
    entries = index.shape[0]
    select = (jnp.arange(width, dtype=jnp.int32)[:, None] == jnp.asarray(index).reshape(1, -1)).astype(chosen.dtype)
    picked = jnp.dot(chosen.reshape(share * kpoints, width), select)
    picked = picked.reshape(share, kpoints, entries, ROWS)
    cut = 2 * CBANDS
    electron = picked[:, :, :cut, None, :] * jnp.asarray(electron_mask, chosen.dtype)
    hole = picked[:, :, cut:, None, :] * jnp.asarray(hole_mask, chosen.dtype)
    return jnp.concatenate(
        [
            electron.reshape(share, kpoints, 2 * BANDS, ROWS),
            hole.reshape(share, kpoints, 2 * BANDS, ROWS),
        ],
        axis=2,
    )


def rate_kernel(omega_ref, gain_ref, own_ref, far_ref, own_e_ref, far_e_ref, rate_ref, mixed):
    pair = pl.program_id(0)
    kpoints = gain_ref.shape[1]
    columns = own_ref.shape[-1]
    trans = kpoints * BANDS

    def mix(step, carry):
        parts = []
        for offset in range(2):
            k = step * 2 + offset
            parts.append(
                lax.dot_general(
                    gain_ref[0, k], own_ref[0, k], (((0,), (0,)), ((), ())), preferred_element_type=jnp.float32
                )
            )
        start = pl.multiple_of(step * 2 * BANDS, 2 * BANDS)
        for u in range(MODES):
            for p in range(2):
                low = (u * 2 + p) * BANDS
                both = jnp.concatenate([part[low : low + BANDS] for part in parts], axis=0)
                mixed[u, pl.ds(start, 2 * BANDS), p * columns : (p + 1) * columns] = both.astype(jnp.bfloat16)
        return carry

    lax.fori_loop(0, kpoints // 2, mix, 0)
    far_real = far_ref[:, 0, 0].reshape(-1, trans)
    far_imag = far_ref[:, 0, 1].reshape(-1, trans)
    gap = far_e_ref[0] - own_e_ref[0]

    def mode(u, total):
        first = mixed[u]
        second = jnp.concatenate([first[:, columns:], -first[:, :columns]], axis=1)
        coupled = jnp.dot(far_real, first, preferred_element_type=jnp.float32)
        coupled += jnp.dot(far_imag, second, preferred_element_type=jnp.float32)
        real, imag = coupled[:, :columns], coupled[:, columns:]
        scaled = (gap - omega_ref[pair, u]) / broadening
        power = (real * real + imag * imag) / (1.0 + scaled * scaled)
        return total + jnp.sum(power, axis=0, keepdims=True)

    rate_ref[0] = lax.fori_loop(0, MODES, mode, jnp.zeros((1, columns), jnp.float32))


def pair_rates(omega, gain, own, far, own_e, far_e):
    share, kpoints, depth, rows = gain.shape
    columns = own.shape[-1]
    parts, trans = far.shape[0], far.shape[-1]
    excitons = parts * far.shape[3]
    flops = 2 * share * (kpoints * depth * rows * columns + excitons * 4 * trans * MODES * columns)
    return pl.pallas_call(
        rate_kernel,
        grid=(share,),
        in_specs=[
            pl.BlockSpec(memory_space=pltpu.SMEM),
            pl.BlockSpec((1, kpoints, depth, rows), lambda i: (i, 0, 0, 0)),
            pl.BlockSpec((1, kpoints, depth, columns), lambda i: (i, 0, 0, 0)),
            pl.BlockSpec((parts, 1, 2, far.shape[3], trans), lambda i: (0, i, 0, 0, 0)),
            pl.BlockSpec((1, 1, columns), lambda i: (i, 0, 0)),
            pl.BlockSpec((1, excitons, 1), lambda i: (i, 0, 0)),
        ],
        out_specs=pl.BlockSpec((1, 1, columns), lambda i: (i, 0, 0)),
        out_shape=jax.ShapeDtypeStruct((share, 1, columns), jnp.float32),
        scratch_shapes=[pltpu.VMEM((MODES, trans, 2 * columns), jnp.bfloat16)],
        compiler_params=pltpu.CompilerParams(vmem_limit_bytes=56 * 1024 * 1024),
        cost_estimate=pl.CostEstimate(flops=flops, bytes_accessed=2 * (gain.size + own.size + far.size), transcendentals=0),
    )(omega, gain, own, far, own_e, far_e)


def shards(coeffs, energies, g_coupling, omega, pairs, counts, blocks):
    worker = lax.axis_index("wide")
    part = lax.axis_index("narrow")
    workers = lax.axis_size("wide")
    owned, _, columns, trans = coeffs.shape
    kpoints = g_coupling.shape[1]
    momenta = owned * workers
    slots = pairs.shape[0]
    excitons = blocks.shape[1]

    small = jnp.concatenate([energies.astype(jnp.float32).reshape(-1), pairs.astype(jnp.float32).reshape(-1)])
    small = lax.all_gather(small, ("wide", "narrow"), axis=0, tiled=False)
    small = small.reshape(workers, -1, small.shape[-1])
    levels = small[:, :, : owned * columns].reshape(workers, -1, owned, columns)
    levels = levels.transpose(0, 2, 1, 3).reshape(momenta, excitons)
    all_pairs = small[:, 0, owned * columns :].astype(jnp.int32).reshape(workers * slots, 2)

    ends = jnp.sum(jnp.where(jnp.arange(workers)[:, None] <= jnp.arange(workers)[None, :], counts[:, None], 0), axis=0)
    live = jnp.arange(momenta)
    holder = jnp.sum((ends[None, :] <= live[:, None]).astype(jnp.int32), axis=1)
    holder = jnp.minimum(holder, workers - 1)
    slot = holder * slots + live - (jnp.take(ends, holder) - jnp.take(counts, holder))
    live_pairs = jnp.take(all_pairs, jnp.clip(slot, 0, workers * slots - 1), axis=0)
    live_home = live_pairs[:, 0]
    mine = lax.dynamic_slice_in_dim(live_pairs, worker * owned, owned, 0)
    home, shift = mine[:, 0], mine[:, 1]
    far_index = (home + shift) % momenta

    tables = lax.all_gather(g_coupling, "narrow", axis=0, tiled=True)
    gain = expand_coupling(jnp.take(tables, shift, axis=0))
    frequency = jnp.take(omega, shift, axis=0)

    whole = lax.all_gather(coeffs, "wide", axis=0, tiled=True)
    far = lax.all_gather(jnp.take(whole, far_index, axis=0), "narrow", axis=0, tiled=False)
    own = jnp.take(whole, home, axis=0).reshape(owned, 2, columns, kpoints, CBANDS, VBANDS)
    by_electron = own.transpose(0, 3, 1, 4, 5, 2).reshape(owned, kpoints, 2 * BANDS, columns)
    by_hole = own.transpose(0, 3, 1, 5, 4, 2).reshape(owned, kpoints, 2 * BANDS, columns)
    own = jnp.concatenate([by_electron, by_hole], axis=2)

    own_e = lax.dynamic_slice_in_dim(jnp.take(levels, home, axis=0), part * columns, columns, 1)
    far_e = jnp.take(levels, far_index, axis=0)
    rates = pair_rates(frequency, gain, own, far, own_e[:, None, :], far_e[:, :, None])

    rates = lax.all_gather(rates.reshape(owned, columns), ("wide", "narrow"), axis=0, tiled=False)
    rates = rates.reshape(workers, -1, owned, columns).transpose(0, 2, 1, 3).reshape(momenta, excitons)
    local = worker * owned + jnp.arange(owned)
    chosen = (live_home[None, :] == local[:, None]).astype(jnp.float32)
    total = jnp.sum(chosen[:, :, None] * rates[None, :, :], axis=1)
    margin = 3
    widened = jnp.pad(total, ((0, 0), (margin, margin)))
    padded_labels = jnp.pad(blocks, ((0, 0), (margin, margin)), constant_values=-1)
    widened = lax.dynamic_slice_in_dim(widened, part * columns, columns + 2 * margin, 1)
    near_labels = lax.dynamic_slice_in_dim(padded_labels, part * columns, columns + 2 * margin, 1)
    my_labels = near_labels[:, margin : margin + columns]
    upper = jnp.zeros((owned, columns), jnp.float32)
    lower = jnp.zeros((owned, columns), jnp.float32)
    for offset in range(2 * margin + 1):
        same = (near_labels[:, offset : offset + columns] == my_labels).astype(jnp.float32)
        upper += same * widened[:, offset : offset + columns]
        lower += same
    return upper / lower


def solution(mesh):
    in_specs = (
        P(("groups", "wide"), None, "narrow", None),
        P(("groups", "wide"), "narrow"),
        P(("groups", "narrow"), None, None),
        P("groups", None),
        P(("groups", "wide"), None),
        P("groups"),
        P(("groups", "wide"), None),
    )
    out_specs = P(("groups", "wide"), "narrow")
    return jax.shard_map(shards, mesh=mesh, in_specs=in_specs, out_specs=out_specs, check_vma=False)
```

time: 938 us -> 287 us (0.31)
  matrix products: 315 us -> 8.08 us
  other arithmetic: 214 us -> 21.2 us
  waiting for transfers between devices: 216 us -> 37.7 us
  blocking collectives: 58.8 us -> 126 us
  local copies, waits for them, and re-layouts: 90.2 us -> 35.8 us
  Pallas kernels: 0 us -> 43 us
  loops' own time: 24 us -> 0 us
    dot_general x37 -> x1, matrix products: 315 us -> 8.08 us  [expand_coupling(): picked = jnp.dot(chosen.reshape(share * kpoints, width), select)]
    concatenate x5 -> x2, other arithmetic: 191 us -> 10.5 us  [the longest x1 8.56 us: expand_coupling(): jnp.concatenate([electron.reshape(share, kpoints, 2 * BANDS, ROWS), hole....]
    all_gather x2, waiting for transfers between devices: 211 us -> 37 us  [the longest x1 37 us: shards(): lax.all_gather(jnp.take(whole, far_index, axis=0), 'narrow', axis=0, tile...]
    unnamed x0 -> x1, blocking collectives: none -> 64.3 us
    pallas_call x0 -> x1, Pallas kernels: none -> 43 us  [pair_rates(): pl.pallas_call(rate_kernel, grid=(share,), in_specs=[pl.BlockSpec(memory_...]
    convert_element_type x8 -> x2, local copies, waits for them, and re-layouts: 38 us -> 0.17 us  [the longest x1 0.1 us: shards(): pairs.astype(jnp.float32).reshape(-1)]
    another operation x1 -> x0, loops' own time: 24 us -> none  [shards(): lax.map(one_slot, (own_a, own_e, far_a, far_e, coupling_rows, shift_index))]
    mul x0 -> x3, local copies, waits for them, and re-layouts: none -> 16.7 us  [the longest x2 15.9 us: expand_coupling(): picked[:, :, :cut, None, :] * jnp.asarray(electron_mask, chosen.dtype)]
  transfers between devices with their start and end apart: 4 -> 2, of which waited for: 3 -> 1; matrix products, arithmetic and copies ran while one was open for 2% -> 21% of each run, Pallas kernels for 0% -> 0%
where the time goes in v1:
time: 287 us; the launch traced here: 286 us
  blocking collectives  126 us (44%)
  Pallas kernels  43 us (15%)
  waiting for transfers between devices  37.7 us (13%)
  local copies, waits for them, and re-layouts  35.8 us (12%)
  other arithmetic  21.2 us (7%)
  between operations  14.3 us (5%)
  matrix products  8.08 us (3%)
    unnamed x1, blocking collectives  64.3 us
    pallas_call x1, Pallas kernels, pair_rates(): pl.pallas_call(rate_kernel, grid=(share,), in_specs=[pl.BlockSpec(memory_...  43 us
    all_gather x1, waiting for transfers between devices, shards(): lax.all_gather(jnp.take(whole, far_index, axis=0), 'narrow', axis=0, tile...  37 us
    all_gather x1, blocking collectives, shards(): lax.all_gather(rates.reshape(owned, columns), ('wide', 'narrow'), axis=0,...  31.6 us
    all_gather x1, blocking collectives, shards(): tables = lax.all_gather(g_coupling, 'narrow', axis=0, tiled=True)  30.2 us
    mul x2, local copies, waits for them, and re-layouts, expand_coupling(): picked[:, :, :cut, None, :] * jnp.asarray(electron_mask, chosen.dtype)  15.9 us
    concatenate x1, other arithmetic, expand_coupling(): jnp.concatenate([electron.reshape(share, kpoints, 2 * BANDS, ROWS), hole....  8.56 us
    dot_general x1, matrix products, expand_coupling(): picked = jnp.dot(chosen.reshape(share * kpoints, width), select)  8.08 us
  transfers between devices with their start and end apart: 2, of which 1 were waited for; matrix products, arithmetic and copies ran while one was open for 21% of the time, Pallas kernels for 0%

profile of v1, /device:TPU:0, one launch (start us, length us, event | category | flops | bytes accessed | tf_op | source)
XLA Modules:
  0.0 286.2 jit_solution(16302497346154171647)
XLA Ops:
  6.5 0.0 copy-start
  6.5 0.0 all-gather.6.cloned.1.call-start
  6.5 0.7 all-gather.6.cloned.1.call-update
  7.3 0.0 all-gather.8.cloned.1.call-start
  7.3 0.7 select_reduce_fusion
  8.1 0.1 convert_reduce_fusion
  8.2 1.3 gather_fusion.4
  9.5 0.6 gather_fusion.3
  10.1 0.7 convert_element_type.45
  10.8 0.1 copy.46
  10.9 0.1 reshape.129
  11.0 1.2 dynamic-slice
  12.9 0.7 bitcast_convert_fusion
  13.5 0.1 maximum_dynamic-update-slice_fusion
  13.6 64.3 %all-reduce.2 = f32[4224]{0:T(1024)S(1)} all-reduce(f32[4224]{0:T(1024)S(1)} %maximum_dynamic-update-slice_fusion), channel_id=2, replica_groups=mesh['groups'=2,'wide'=4,'narrow'=4] {'wide','narrow'}, use_global_device_ids=true, to_apply=%add.2 | all-reduce | flops 4224 | bytes 33792
  77.9 0.1 reshape.130
  78.0 0.0 copy-start.4
  78.0 0.1 convert_element_type.47
  78.2 0.6 gather_fusion
  78.7 0.1 broadcast_select_fusion.2
  78.8 0.2 slice_reduce_fusion.2
  79.1 0.0 all-gather.6.cloned.1.call-done
  79.1 3.4 %gather_fusion.6 = bf16[2,2,128,1536]{3,2,1,0:T(8,128)(2,1)S(1)} fusion(bf16[8,2,128,1536]{3,2,1,0:T(8,128)(2,1)} %all-gather.6.cloned.1.call-done, s32[1024]{0:T(1024)S(1)} %pad_clamp_fusion), kind=kCustom, calls=%fused_computation.4.clone | custom fusion | bytes 3145736 | tf_op jit(solution)/shard_map/jit(_take)/gather | solution.py:160
  82.5 1.4 broadcast_select_fusion
  84.0 0.0 all-gather.8.cloned.1.call-update
  84.0 0.0 copy-done.3
  84.0 30.2 %all_gather.23 = bf16[8,64,936]{2,1,0:T(8,128)(2,1)S(1)} all-gather(bf16[2,64,936]{2,1,0:T(8,128)(2,1)S(1)} %copy-done.3), channel_id=1, replica_groups=mesh['groups'=2,'wide'=4,'narrow'=4] {'narrow'}, dimensions={0}, use_global_device_ids=true | all-gather | bytes 1198080 | tf_op jit(solution)/shard_map/all_gather | solution.py:155
  114.2 0.6 gather_fusion.2
  114.8 0.2 and_reduce_fusion
  115.0 0.0 copy-done.8
  115.0 8.1 %fusion.1 = bf16[2,64,20,432]{3,1,2,0:T(8,128)(2,1)S(1)} fusion(s32[20,432]{1,0:T(8,128)S(1)} %copy-done.8, bf16[2,64,936]{2,1,0:T(8,128)(2,1)S(1)} %gather_fusion.2, pred[2]{0:T(512)(128)(4,1)S(1)} %and_reduce_fusion), kind=kOutput, calls=%fused_computation.11 | convolution fusion | flops 2078489088 | bytes 2486018 | tf_op jit(solution)/shard_map/dot_general | solution.py:47
  123.1 0.1 slice.105
  123.2 0.2 slice.104
  123.3 0.0 copy-done.4
  123.4 0.6 gather_fusion.1
  123.9 0.9 copy.47
  124.8 5.4 %mul.86 = bf16[2,64,12,4,432]{4,3,2,1,0:T(4,128)(2,1)} broadcast(bf16[2,64,12,432]{3,2,1,0:T(8,128)(2,1)S(1)} %copy.47), dimensions={0,1,2,4} | broadcast | bytes 6635520 | tf_op jit(solution)/shard_map/mul | solution.py:50
  130.2 10.6 %mul.87 = bf16[2,64,48,432]{3,2,1,0:T(8,128)(2,1)} reshape(bf16[2,64,12,4,432]{4,3,2,1,0:T(4,128)(2,1)} %mul.86) | data formatting | bytes 10616832 | tf_op jit(solution)/shard_map/mul | solution.py:50
  140.8 0.0 slice-done
  140.8 0.6 gather_fusion.8
  141.4 0.6 gather_fusion.7
  142.0 0.1 select_bitcast_fusion
  142.0 1.0 copy.54.far_e_ref
  143.1 0.1 slice_reduce_fusion
  143.2 0.6 fusion.10
  143.8 0.1 compare_convert_fusion
  143.8 0.6 broadcast_select_fusion.3.omega_ref
  144.5 0.8 mul.91
  145.3 0.6 copy-done.2
  145.9 4.0 %copy_multiply_fusion = (bf16[2,64,48,432]{3,2,1,0:T(8,128)(2,1)S(1)}, bf16[2,64,48,432]{3,2,1,0:T(8,128)(2,1)S(1)}) fusion(bf16[2,64,48,432]{3,1,2,0:T(8,128)(2,1)S(1)} %bitcast.39, bf16[48,432]{1,0:T(8,128)(2,1)S(1)} %copy-done.5, bf16[2,64,48,432]{3,2,1,0:T(8,128)(2,1)S(1)} %copy-done.2, bf16[48,432]{1,0:T(8,128)(2,1)S(1)} %copy-done.6), kind=kLoop, calls=%fused_computation.14 | loop fusion | flops 5308416 | bytes 21316608 | tf_op jit(solution)/shard_map/mul | solution.py:51
  149.9 8.6 %pad_maximum_fusion.gain_ref = bf16[2,64,96,432]{3,2,1,0:T(8,128)(2,1)} fusion(bf16[2,64,48,432]{3,2,1,0:T(8,128)(2,1)S(1)} %get-tuple-element.16, bf16[2,64,48,432]{3,2,1,0:T(8,128)(2,1)S(1)} %get-tuple-element.17), kind=kLoop, calls=%fused_computation.13 | loop fusion | flops 21233664 | bytes 21233664 | tf_op jit(solution)/shard_map/concatenate | solution.py:52
  158.4 3.5 %gather_fusion.5 = bf16[2,2,128,1536]{3,2,1,0:T(8,128)(2,1)S(1)} fusion(bf16[8,2,128,1536]{3,2,1,0:T(8,128)(2,1)} %all-gather.6.cloned.1.call-done, s32[1024]{0:T(1024)S(1)} %pad_clamp_fusion.1), kind=kCustom, calls=%fused_computation.1.clone | custom fusion | bytes 3145736 | tf_op jit(solution)/shard_map/jit(_take)/gather | solution.py:161
  161.9 0.2 broadcast_select_fusion.1
  162.2 0.9 copy.49
  163.1 0.4 copy.51
  163.5 1.0 copy.52
  164.5 0.5 copy.50
  165.0 1.9 pad_maximum_fusion.1.own_ref
  167.0 37.0 %all-gather.8.cloned.1.call-done = bf16[8,2,128,1536]{3,2,1,0:T(8,128)(2,1)} async-done(((bf16[2,2,128,1536]{3,2,1,0:T(8,128)(2,1)}), bf16[8,2,128,1536]{3,2,1,0:T(8,128)(2,1)}) %all-gather.8.cloned.1.call-update) | async-done | bytes 6291472 | tf_op jit(solution)/shard_map/all_gather | solution.py:160
  204.0 43.0 %shard_map.100 = f32[2,1,128]{2,1,0:T(1,128)} custom-call(f32[2,9]{1,0:T(2,128)} %broadcast_select_fusion.3.omega_ref, bf16[2,64,96,432]{3,2,1,0:T(8,128)(2,1)} %pad_maximum_fusion.gain_ref, bf16[2,64,96,128]{3,2,1,0:T(8,128)(2,1)} %pad_maximum_fusion.1.own_ref, bf16[4,2,2,128,1536]{4,3,2,1,0:T(8,128)(2,1)} %bitcast.51, f32[2,1,128]{2,1,0:T(1,128)} %bitcast.50, ...), custom_call_target="tpu_custom_call" | custom-call | flops 15854469120 | bytes 20054016 | tf_op jit(solution)/shard_map/pallas_call | solution.py:108
  247.0 31.6 %all-gather.2 = f32[32,1,128]{2,1,0:T(1,128)S(1)} all-gather(f32[2,1,128]{2,1,0:T(1,128)} %shard_map.100), channel_id=4, replica_groups=mesh['groups'=2,'wide'=4,'narrow'=4] {'wide','narrow'}, dimensions={0}, use_global_device_ids=true | all-gather | bytes 17408 | tf_op jit(solution)/shard_map/all_gather | solution.py:170
  278.6 0.1 multiply_reduce_fusion
  278.7 0.7 fusion.13
  279.4 0.0 copy-done.1
  (28 shorter events, 0.1 us)
Async XLA Ops:
  6.5 116.8 %copy-start = (f32[8,9]{1,0:T(8,128)S(1)}, f32[8,9]{1,0:T(8,128)}, u32[]{:S(2)}) copy-start(f32[8,9]{1,0:T(8,128)} %param.19) | copy-start | bytes 868
  6.5 108.5 %copy-start.8 = (s32[20,432]{1,0:T(8,128)S(1)}, s32[20,432]{1,0:T(8,128)}, u32[]{:S(2)}) copy-start(s32[20,432]{1,0:T(8,128)} %constant.128.clone) | copy-start | bytes 103684
  6.5 77.5 %copy-start.3 = (bf16[2,64,936]{2,1,0:T(8,128)(2,1)S(1)}, bf16[2,64,936]{2,1,0:T(8,128)(2,1)}, u32[]{:S(2)}) copy-start(bf16[2,64,936]{2,1,0:T(8,128)(2,1)} %param.18) | copy-start | bytes 718852
  6.5 72.5 %all-gather.6.cloned.1.call-start = ((), (), s32[]{:S(2)}) async-start(), calls=%async_computation | async-start | bytes 7864320 | tf_op jit(solution)/shard_map/all_gather | solution.py:159
  7.3 196.7 %all-gather.8.cloned.1.call-start = ((), (), s32[]{:S(2)}) async-start(), calls=%async_computation.1 | async-start | bytes 7864320 | tf_op jit(solution)/shard_map/all_gather | solution.py:160
  78.0 45.3 %copy-start.4 = (f32[4,4,264]{2,1,0:T(4,128)}, f32[4,4,264]{2,1,0:T(4,128)S(1)}, u32[]{:S(2)}) copy-start(f32[4,4,264]{2,1,0:T(4,128)S(1)} %reshape.130) | copy-start | bytes 50692
  130.2 10.6 %slice-start = ((f32[4,4,264]{2,1,0:T(4,128)}), f32[4,4,256]{2,1,0:T(4,128)S(1)}, s32[]{:S(2)}) async-start(f32[4,4,264]{2,1,0:T(4,128)} %copy-done.4), calls=%async_computation.2 | async-start | bytes 32768 | tf_op jit(solution)/shard_map/slice | solution.py:140
  140.8 4.5 %copy-start.5 = (bf16[48,432]{1,0:T(8,128)(2,1)S(1)}, bf16[48,432]{1,0:T(8,128)(2,1)}, u32[]{:S(2)}) copy-start(bf16[48,432]{1,0:T(8,128)(2,1)} %constant.141) | copy-start | bytes 124420
  140.8 4.5 %copy-start.6 = (bf16[48,432]{1,0:T(8,128)(2,1)S(1)}, bf16[48,432]{1,0:T(8,128)(2,1)}, u32[]{:S(2)}) copy-start(bf16[48,432]{1,0:T(8,128)(2,1)} %constant.140) | copy-start | bytes 124420
  143.1 2.8 copy-start.2
  204.0 74.7 %copy-start.7 = (s32[2,512]{1,0:T(2,128)S(1)}, s32[2,512]{1,0:T(2,128)}, u32[]{:S(2)}) copy-start(s32[2,512]{1,0:T(2,128)} %param.22) | copy-start | bytes 12292
  204.0 75.4 %copy-start.1 = (f32[8,9]{1,0:T(8,128)S(1)}, f32[8,9]{1,0:T(8,128)}, u32[]{:S(2)}) copy-start(f32[8,9]{1,0:T(8,128)} %param.19) | copy-start | bytes 868
Sparse Core Ops, SparseCore 0:
  8.9 49.4 all-gather.5
  84.1 119.7 all-gather.7

commit v2 on v1

v2 whole, which is shorter than its diff:
```python
import functools

import jax
import jax.numpy as jnp
import numpy as np
from jax import lax
from jax.experimental import pallas as pl
from jax.experimental.pallas import tpu as pltpu
from jax.sharding import PartitionSpec as P

MODES = 9
CBANDS = 6
VBANDS = 4
BANDS = CBANDS * VBANDS
ROWS = MODES * 2 * BANDS

broadening = 0.1
MESH = pl.DeviceIdType.MESH


def expansion_tables():
    u, pout, c, v = np.unravel_index(np.arange(ROWS), (MODES, 2, CBANDS, VBANDS))
    cut = 2 * MODES * CBANDS * CBANDS
    index, mask = [], []
    for pin in range(2):
        part = pout ^ pin
        sign = np.where((pout == 0) & (pin == 1), -1.0, 1.0)
        for d in range(CBANDS):
            index.append(((part * MODES + u) * CBANDS + c) * CBANDS + d)
            mask.append(np.stack([sign * (v == other) for other in range(VBANDS)]))
    electron_mask = np.stack(mask)
    mask = []
    for pin in range(2):
        part = pout ^ pin
        sign = np.where((pout == 0) & (pin == 1), 1.0, -1.0)
        for w in range(VBANDS):
            index.append(cut + ((part * MODES + u) * VBANDS + v) * VBANDS + w)
            mask.append(np.stack([sign * (c == other) for other in range(CBANDS)]))
    hole_mask = np.stack(mask)
    return np.stack(index).astype(np.int32), electron_mask, hole_mask


def spread_tables():
    electron = np.arange(2 * CBANDS * VBANDS) // VBANDS
    pin, _, w = np.unravel_index(np.arange(2 * CBANDS * VBANDS), (2, CBANDS, VBANDS))
    hole = 2 * CBANDS + pin * VBANDS + w
    source = np.concatenate([electron, hole])
    return (source[:, None] == np.arange(2 * (CBANDS + VBANDS))[None, :]).astype(np.float32)


def pick_coupling(chosen):
    index = expansion_tables()[0]
    share, kpoints, width = chosen.shape
    select = (jnp.arange(width, dtype=jnp.int32)[:, None] == jnp.asarray(index).reshape(1, -1)).astype(chosen.dtype)
    picked = jnp.dot(chosen.reshape(share * kpoints, width), select)
    return picked.reshape(share, kpoints, index.shape[0], ROWS)


def greet(workers, parts):
    worker, part = lax.axis_index("wide"), lax.axis_index("narrow")
    barrier = pltpu.get_barrier_semaphore()
    me = worker * parts + part
    total = workers * parts

    def hello(step, carry):
        other = lax.rem(me + step, total)
        pl.semaphore_signal(
            barrier, inc=1, device_id={"wide": other // parts, "narrow": lax.rem(other, parts)}, device_id_type=MESH
        )
        return carry

    lax.fori_loop(1, total, hello, 0)
    pl.semaphore_wait(barrier, total - 1)


def to_all(workers, parts, source, landing, send_sem, recv_sem, wait):
    worker, part = lax.axis_index("wide"), lax.axis_index("narrow")
    me = worker * parts + part
    total = workers * parts

    def one(step, carry):
        other = lax.rem(me + step, total)
        copy = pltpu.make_async_remote_copy(
            src_ref=source,
            dst_ref=landing.at[me],
            send_sem=send_sem.at[step],
            recv_sem=recv_sem.at[step],
            device_id={"wide": other // parts, "narrow": lax.rem(other, parts)},
            device_id_type=MESH,
        )
        if wait:
            copy.wait()
        else:
            copy.start()
        return carry

    lax.fori_loop(1, total, one, 0)


def exchange_kernel(workers, parts, small_ref, table_ref, small_out, table_out, smalls, tables, s_send, s_recv, t_send, t_recv):
    worker, part = lax.axis_index("wide"), lax.axis_index("narrow")
    me = worker * parts + part
    greet(workers, parts)
    to_all(workers, parts, small_ref, smalls, s_send, s_recv, False)
    copies = []
    for step in range(1, parts):
        copy = pltpu.make_async_remote_copy(
            src_ref=table_ref,
            dst_ref=tables.at[part],
            send_sem=t_send.at[step],
            recv_sem=t_recv.at[step],
            device_id={"narrow": lax.rem(part + step, parts)},
            device_id_type=MESH,
        )
        copy.start()
        copies.append(copy)
    smalls[me] = small_ref[...]
    tables[part] = table_ref[...]
    to_all(workers, parts, small_ref, smalls, s_send, s_recv, True)
    for copy in copies:
        copy.wait()
    small_out[...] = smalls[...]
    table_out[...] = tables[...]


def exchange(workers, parts, small, table):
    total = workers * parts
    return pl.pallas_call(
        functools.partial(exchange_kernel, workers, parts),
        in_specs=[pl.BlockSpec(memory_space=pltpu.VMEM)] * 2,
        out_specs=[pl.BlockSpec(memory_space=pltpu.VMEM)] * 2,
        out_shape=[
            jax.ShapeDtypeStruct((total,) + small.shape, small.dtype),
            jax.ShapeDtypeStruct((parts,) + table.shape, table.dtype),
        ],
        scratch_shapes=[
            pltpu.VMEM((total,) + small.shape, small.dtype),
            pltpu.VMEM((parts,) + table.shape, table.dtype),
            pltpu.SemaphoreType.DMA((total,)),
            pltpu.SemaphoreType.DMA((total,)),
            pltpu.SemaphoreType.DMA((parts,)),
            pltpu.SemaphoreType.DMA((parts,)),
        ],
        compiler_params=pltpu.CompilerParams(
            collective_id=0, has_side_effects=True, vmem_limit_bytes=24 * 1024 * 1024
        ),
        cost_estimate=pl.CostEstimate(flops=0, bytes_accessed=4 * parts * table.size, transcendentals=0),
    )(small, table)


def rate_kernel(
    workers, parts, omega_ref, picked_ref, spread_ref, mask_ref, own_ref, far_ref, own_e_ref, far_e_ref, out_ref,
    near, distant, mixed, rates, gathered, n_send, n_recv, m_send, m_recv, local_sem, r_send, r_recv,
):
    worker, part = lax.axis_index("wide"), lax.axis_index("narrow")
    me = worker * parts + part
    half = parts // 2
    side, place = part // half, lax.rem(part, half)
    share, kpoints = picked_ref.shape[:2]
    columns = own_ref.shape[-1]
    trans = kpoints * BANDS
    width = half * columns

    def near_copy(pair, i):
        return pltpu.make_async_remote_copy(
            src_ref=own_ref.at[pair],
            dst_ref=near.at[pair, place],
            send_sem=n_send.at[pair, i],
            recv_sem=n_recv.at[pair, place],
            device_id={"narrow": side * half + i},
            device_id_type=MESH,
        )

    def far_copy(pair, t):
        return pltpu.make_async_remote_copy(
            src_ref=far_ref.at[pair],
            dst_ref=distant.at[pair, lax.rem(part, 2)],
            send_sem=m_send.at[pair, t],
            recv_sem=m_recv.at[pair, lax.rem(part, 2)],
            device_id={"narrow": t * half + part // 2},
            device_id_type=MESH,
        )

    def near_self(pair):
        return pltpu.make_async_copy(own_ref.at[pair], near.at[pair, place], local_sem.at[pair, 0])

    def far_self(pair):
        return pltpu.make_async_copy(far_ref.at[pair], distant.at[pair, lax.rem(part, 2)], local_sem.at[pair, 1])

    greet(workers, parts)
    for pair in range(share):
        near_self(pair).start()
        for i in range(half):
            pl.when(side * half + i != part)(near_copy(pair, i).start)
        for t in range(2):
            target = t * half + part // 2
            pl.when(target != part)(far_copy(pair, t).start)
            pl.when(target == part)(far_self(pair).start)

    def one_pair(pair, carry):
        for i in range(half):

            @pl.when(side * half + i != part)
            def _():
                pltpu.make_async_remote_copy(
                    src_ref=own_ref.at[pair],
                    dst_ref=near.at[pair, i],
                    send_sem=n_send.at[pair, i],
                    recv_sem=n_recv.at[pair, i],
                    device_id={"narrow": side * half + i},
                    device_id_type=MESH,
                ).wait_recv()

        near_self(pair).wait()

        def mix(step, carry):
            blocks = []
            for offset in range(2):
                k = step * 2 + offset
                spread = jnp.dot(spread_ref[...], picked_ref[pair, k], preferred_element_type=jnp.float32)
                gain = spread.astype(jnp.bfloat16) * mask_ref[...]
                rows = jnp.concatenate([near[pair, i, k] for i in range(half)], axis=1)
                rows = jnp.concatenate([rows, rows], axis=0)
                blocks.append(
                    lax.dot_general(gain, rows, (((0,), (0,)), ((), ())), preferred_element_type=jnp.float32)
                )
            start = pl.multiple_of(step * 2 * BANDS, 2 * BANDS)
            for u in range(MODES):
                for p in range(2):
                    low = (u * 2 + p) * BANDS
                    both = jnp.concatenate([block[low : low + BANDS] for block in blocks], axis=0)
                    mixed[u, pl.ds(start, 2 * BANDS), p * width : (p + 1) * width] = both.astype(jnp.bfloat16)
            return carry

        lax.fori_loop(0, kpoints // 2, mix, 0)

        for s in range(2):

            @pl.when(place * 2 + s != part)
            def _():
                pltpu.make_async_remote_copy(
                    src_ref=far_ref.at[pair],
                    dst_ref=distant.at[pair, s],
                    send_sem=m_send.at[pair, s],
                    recv_sem=m_recv.at[pair, s],
                    device_id={"narrow": place * 2 + s},
                    device_id_type=MESH,
                ).wait_recv()

            pl.when(place * 2 + s == part)(far_self(pair).wait)

        far_rows = distant[pair].reshape(4 * columns, trans)
        gap = far_e_ref[pair] - own_e_ref[pair]

        def mode(u, total):
            coupled = jnp.dot(far_rows, mixed[u], preferred_element_type=jnp.float32)
            coupled = coupled.reshape(2, 2, columns, 2 * width)
            real = coupled[:, 0, :, :width] + coupled[:, 1, :, width:]
            imag = coupled[:, 0, :, width:] - coupled[:, 1, :, :width]
            scaled = (gap - omega_ref[pair, u]) / broadening
            power = (real * real + imag * imag).reshape(2 * columns, width) / (1.0 + scaled * scaled)
            return total + jnp.sum(power, axis=0, keepdims=True)

        rates[pair] = lax.fori_loop(0, MODES, mode, jnp.zeros((1, width), jnp.float32))
        return carry

    lax.fori_loop(0, share, one_pair, 0)
    gathered[me] = rates[...]
    to_all(workers, parts, rates, gathered, r_send, r_recv, False)
    for pair in range(share):
        for i in range(half):
            pl.when(side * half + i != part)(near_copy(pair, i).wait_send)
        for t in range(2):
            pl.when(t * half + part // 2 != part)(far_copy(pair, t).wait_send)
    to_all(workers, parts, rates, gathered, r_send, r_recv, True)
    out_ref[...] = gathered[...]


def pair_rates(workers, parts, omega, picked, own, far, own_e, far_e):
    share, kpoints = picked.shape[:2]
    columns = own.shape[-1]
    trans = far.shape[-1]
    total, width = workers * parts, parts // 2 * columns
    _, electron_mask, hole_mask = expansion_tables()
    hole_mask = hole_mask.reshape(2, VBANDS, CBANDS, ROWS).transpose(0, 2, 1, 3)
    mask = np.concatenate([electron_mask.reshape(2 * BANDS, ROWS), hole_mask.reshape(2 * BANDS, ROWS)])
    flops = 2 * share * (kpoints * 4 * BANDS * ROWS * width + 8 * columns * trans * MODES * width)
    vmem = pl.BlockSpec(memory_space=pltpu.VMEM)
    dma = pltpu.SemaphoreType.DMA
    return pl.pallas_call(
        functools.partial(rate_kernel, workers, parts),
        in_specs=[pl.BlockSpec(memory_space=pltpu.SMEM)] + [vmem] * 7,
        out_specs=vmem,
        out_shape=jax.ShapeDtypeStruct((total, share, 1, width), jnp.float32),
        scratch_shapes=[
            pltpu.VMEM((share, parts // 2) + own.shape[1:], own.dtype),
            pltpu.VMEM((share, 2) + far.shape[1:], far.dtype),
            pltpu.VMEM((MODES, trans, 2 * width), jnp.bfloat16),
            pltpu.VMEM((share, 1, width), jnp.float32),
            pltpu.VMEM((total, share, 1, width), jnp.float32),
            dma((share, parts // 2)),
            dma((share, parts // 2)),
            dma((share, 2)),
            dma((share, 2)),
            dma((share, 2)),
            dma((total,)),
            dma((total,)),
        ],
        compiler_params=pltpu.CompilerParams(
            collective_id=1, has_side_effects=True, vmem_limit_bytes=56 * 1024 * 1024
        ),
        cost_estimate=pl.CostEstimate(flops=flops, bytes_accessed=2 * (picked.size + own.size + far.size), transcendentals=0),
    )(omega, picked, jnp.asarray(spread_tables(), jnp.bfloat16), jnp.asarray(mask, jnp.bfloat16), own, far, own_e, far_e)


def shards(coeffs, energies, g_coupling, omega, pairs, counts, blocks):
    worker = lax.axis_index("wide")
    part = lax.axis_index("narrow")
    workers = lax.axis_size("wide")
    owned, _, columns, trans = coeffs.shape
    kpoints = g_coupling.shape[1]
    momenta = owned * workers
    slots = pairs.shape[0]
    excitons = blocks.shape[1]

    parts = lax.axis_size("narrow")
    small = jnp.concatenate([energies.astype(jnp.float32).reshape(-1), pairs.astype(jnp.float32).reshape(-1)])
    small = jnp.pad(small, (0, -small.shape[0] % 128)).reshape(1, -1)
    small, tables = exchange(workers, parts, small, g_coupling)
    small = small.reshape(workers, parts, small.shape[-1])
    tables = tables.reshape(momenta, kpoints, g_coupling.shape[-1])
    levels = small[:, :, : owned * columns].reshape(workers, -1, owned, columns)
    levels = levels.transpose(0, 2, 1, 3).reshape(momenta, excitons)
    all_pairs = small[:, 0, owned * columns : owned * columns + 2 * slots].astype(jnp.int32).reshape(workers * slots, 2)

    ends = jnp.sum(jnp.where(jnp.arange(workers)[:, None] <= jnp.arange(workers)[None, :], counts[:, None], 0), axis=0)
    live = jnp.arange(momenta)
    holder = jnp.sum((ends[None, :] <= live[:, None]).astype(jnp.int32), axis=1)
    holder = jnp.minimum(holder, workers - 1)
    slot = holder * slots + live - (jnp.take(ends, holder) - jnp.take(counts, holder))
    live_pairs = jnp.take(all_pairs, jnp.clip(slot, 0, workers * slots - 1), axis=0)
    live_home = live_pairs[:, 0]
    mine = lax.dynamic_slice_in_dim(live_pairs, worker * owned, owned, 0)
    home, shift = mine[:, 0], mine[:, 1]
    far_index = (home + shift) % momenta

    picked = pick_coupling(jnp.take(tables, shift, axis=0, mode="clip"))
    frequency = jnp.take(omega, shift, axis=0, mode="clip")

    whole = lax.all_gather(coeffs, "wide", axis=0, tiled=True)
    far = jnp.take(whole, far_index, axis=0, mode="clip")
    own = jnp.take(whole, home, axis=0, mode="clip").reshape(owned, 2, columns, kpoints, BANDS)
    own = own.transpose(0, 3, 1, 4, 2).reshape(owned, kpoints, 2 * BANDS, columns)

    half = parts // 2
    own_e = jnp.take(levels, home, axis=0, mode="clip")
    own_e = lax.dynamic_slice_in_dim(own_e, part // half * half * columns, half * columns, 1)
    far_e = jnp.take(levels, far_index, axis=0, mode="clip")
    far_e = lax.dynamic_slice_in_dim(far_e, part % half * 2 * columns, 2 * columns, 1)
    rates = pair_rates(workers, parts, frequency, picked, own, far, own_e[:, None, :], far_e[:, :, None])

    rates = rates.reshape(workers, 2, half, owned, half * columns).sum(axis=2)
    rates = rates.transpose(0, 2, 1, 3).reshape(momenta, excitons)
    local = worker * owned + jnp.arange(owned)
    chosen = (live_home[None, :] == local[:, None]).astype(jnp.float32)
    total = jnp.sum(chosen[:, :, None] * rates[None, :, :], axis=1)
    margin = 3
    widened = jnp.pad(total, ((0, 0), (margin, margin)))
    padded_labels = jnp.pad(blocks, ((0, 0), (margin, margin)), constant_values=-1)
    widened = lax.dynamic_slice_in_dim(widened, part * columns, columns + 2 * margin, 1)
    near_labels = lax.dynamic_slice_in_dim(padded_labels, part * columns, columns + 2 * margin, 1)
    my_labels = near_labels[:, margin : margin + columns]
    upper = jnp.zeros((owned, columns), jnp.float32)
    lower = jnp.zeros((owned, columns), jnp.float32)
    for offset in range(2 * margin + 1):
        same = (near_labels[:, offset : offset + columns] == my_labels).astype(jnp.float32)
        upper += same * widened[:, offset : offset + columns]
        lower += same
    return upper / lower


def solution(mesh):
    in_specs = (
        P(("groups", "wide"), None, "narrow", None),
        P(("groups", "wide"), "narrow"),
        P(("groups", "narrow"), None, None),
        P("groups", None),
        P(("groups", "wide"), None),
        P("groups"),
        P(("groups", "wide"), None),
    )
    out_specs = P(("groups", "wide"), "narrow")
    return jax.shard_map(shards, mesh=mesh, in_specs=in_specs, out_specs=out_specs, check_vma=False)
```

time: 287 us -> 168 us (0.59)
  blocking collectives: 126 us -> 0 us
  Pallas kernels: 43 us -> 116 us
  waiting for transfers between devices: 37.7 us -> 7.25 us
  other arithmetic: 21.2 us -> 1.46 us
  local copies, waits for them, and re-layouts: 35.8 us -> 20.9 us
    pallas_call x1 -> x2, Pallas kernels: 43 us -> 116 us  [the longest x1 90.6 us: pair_rates(): pl.pallas_call(functools.partial(rate_kernel, workers, parts), in_specs=[...]
    unnamed x1 -> x0, blocking collectives: 64.3 us -> none
    all_gather x2 -> x0, blocking collectives: 61.8 us -> none  [the longest x1 31.6 us: shards(): lax.all_gather(rates.reshape(owned, columns), ('wide', 'narrow'), axis=0,...]
    all_gather x1 -> x0, waiting for transfers between devices: 37 us -> none  [shards(): lax.all_gather(jnp.take(whole, far_index, axis=0), 'narrow', axis=0, tile...]
    mul x3 -> x0, local copies, waits for them, and re-layouts: 16.7 us -> none  [the longest x2 15.9 us: expand_coupling(): picked[:, :, :cut, None, :] * jnp.asarray(electron_mask, chosen.dtype)]
    concatenate x2 -> x1, other arithmetic: 10.5 us -> 0.01 us  [shards(): jnp.concatenate([energies.astype(jnp.float32).reshape(-1), pairs.astype(j...]
    all_gather x1, waiting for transfers between devices: 0.02 us -> 6.57 us  [shards(): whole = lax.all_gather(coeffs, 'wide', axis=0, tiled=True)]
    mul x1 -> x0, other arithmetic: 4 us -> none  [expand_coupling(): hole = picked[:, :, cut:, None, :] * jnp.asarray(hole_mask, chosen.dtype)]
  transfers between devices with their start and end apart: 2 -> 1, of which waited for: 1 -> 1; matrix products, arithmetic and copies ran while one was open for 21% -> 11% of each run, Pallas kernels for 0% -> 15%
where the time goes in v2:
time: 168 us
  Pallas kernels  116 us (69%)
  local copies, waits for them, and re-layouts  20.9 us (12%)
  between operations  13.7 us (8%)
  matrix products  7.92 us (5%)
  waiting for transfers between devices  7.25 us (4%)
    pallas_call x1, Pallas kernels, pair_rates(): pl.pallas_call(functools.partial(rate_kernel, workers, parts), in_specs=[...  90.6 us
    pallas_call x1, Pallas kernels, exchange(): pl.pallas_call(functools.partial(exchange_kernel, workers, parts), in_spe...  25.7 us
    dot_general x1, matrix products, pick_coupling(): picked = jnp.dot(chosen.reshape(share * kpoints, width), select)  7.92 us
    all_gather x1, waiting for transfers between devices, shards(): whole = lax.all_gather(coeffs, 'wide', axis=0, tiled=True)  6.57 us
    gather x1, local copies, waits for them, and re-layouts, shards(): far = jnp.take(whole, far_index, axis=0, mode='clip')  4.56 us
    gather x2, local copies, waits for them, and re-layouts, shards(): jnp.take(whole, home, axis=0, mode='clip')  4.33 us
  transfers between devices with their start and end apart: 1, of which 1 were waited for; matrix products, arithmetic and copies ran while one was open for 11% of the time, Pallas kernels for 15%

profile of v2, /device:TPU:0, one launch (start us, length us, event | category | flops | bytes accessed | tf_op | source)
XLA Modules:
  0.0 167.5 jit_solution(16404356382641294732)
XLA Ops:
  6.5 0.0 copy-start
  6.5 0.0 copy-start.2
  6.5 0.0 copy-start.4
  6.5 0.0 copy-start.5
  6.5 0.0 copy-start.1
  6.5 0.0 all-gather.2.cloned.1.call-start
  6.6 0.7 all-gather.2.cloned.1.call-update
  7.3 0.0 copy-start.6
  7.3 0.0 copy-done.2
  7.3 0.1 select_reduce_fusion
  7.4 0.1 convert_reduce_fusion
  7.5 0.6 gather_fusion.7
  8.2 0.6 gather_fusion.8
  8.8 0.0 copy-done.4
  8.8 0.1 copy.44
  8.9 0.1 reshape.97
  9.0 0.0 copy-done.5
  9.0 0.0 copy-done.1
  9.0 25.7 %shard_map.100 = (f32[16,1,384]{2,1,0:T(1,128)S(1)}, bf16[4,2,64,936]{3,2,1,0:T(8,128)(2,1)S(1)}) custom-call(f32[1,384]{1,0:T(1,128)S(1)} %reshape.98.small_ref, bf16[2,64,936]{2,1,0:T(8,128)(2,1)S(1)} %copy-done.1), custom_call_target="tpu_custom_call" | custom-call | bytes 1916928 | tf_op jit(solution)/shard_map/pallas_call | solution.py:128
  34.8 0.1 reduce
  34.9 0.1 convert_element_type.49
  35.0 0.6 gather_fusion
  35.6 0.1 broadcast_select_fusion
  35.7 0.2 fusion.26
  35.9 0.6 gather_fusion.2
  36.5 0.0 copy-done
  36.5 1.1 gather_fusion.1
  37.6 0.6 gather_fusion.6
  38.2 0.6 gather_fusion.5
  38.7 0.6 broadcast_in_dim.51.own_e_ref
  39.3 0.9 copy.50.far_e_ref
  40.2 0.0 copy-done.6
  40.2 7.9 %fusion.1 = bf16[2,64,20,432]{3,1,2,0:T(8,128)(2,1)S(1)} fusion(s32[20,432]{1,0:T(8,128)S(1)} %copy-done.6, bf16[2,64,936]{2,1,0:T(8,128)(2,1)S(1)} %gather_fusion.2), kind=kOutput, calls=%fused_computation.11 | convolution fusion | flops 2078369280 | bytes 2486016 | tf_op jit(solution)/shard_map/dot_general | solution.py:55
  48.1 3.2 %copy.49.picked_ref = bf16[2,64,20,432]{3,2,1,0:T(8,128)(2,1)} copy(bf16[2,64,20,432]{3,1,2,0:T(8,128)(2,1)S(1)} %fusion.1) | data formatting | bytes 4423680 | tf_op jit(solution)/shard_map/dot_general | solution.py:55
  51.3 0.1 slice_reduce_fusion
  51.5 0.1 compare_convert_fusion
  51.5 6.6 %all-gather.2.cloned.1.call-done = bf16[8,2,128,1536]{3,2,1,0:T(8,128)(2,1)} async-done(((bf16[2,2,128,1536]{3,2,1,0:T(8,128)(2,1)}), bf16[8,2,128,1536]{3,2,1,0:T(8,128)(2,1)}) %all-gather.2.cloned.1.call-update) | async-done | bytes 6291472 | tf_op jit(solution)/shard_map/all_gather | solution.py:350
  58.1 3.4 %gather_fusion.3 = bf16[2,2,128,1536]{3,2,1,0:T(8,128)(2,1)S(1)} fusion(bf16[8,2,128,1536]{3,2,1,0:T(8,128)(2,1)} %all-gather.2.cloned.1.call-done, s32[1024]{0:T(1024)S(1)} %get-tuple-element.16), kind=kCustom, calls=%fused_computation.5 | custom fusion | bytes 3145736 | tf_op jit(solution)/shard_map/jit(_take)/gather | solution.py:352
  61.5 0.9 copy.46
  62.4 1.4 copy.47
  63.9 4.6 %gather_fusion.4 = bf16[2,2,128,1536]{3,2,1,0:T(8,128)(2,1)} fusion(bf16[8,2,128,1536]{3,2,1,0:T(8,128)(2,1)} %all-gather.2.cloned.1.call-done, s32[1024]{0:T(1024)S(1)} %get-tuple-element.15), kind=kCustom, calls=%fused_computation.6 | custom fusion | bytes 3145736 | tf_op jit(solution)/shard_map/jit(_take)/gather | solution.py:351
  68.4 0.0 copy-start.3
  68.5 90.6 %shard_map.101 = f32[16,2,1,256]{3,2,1,0:T(1,128)} custom-call(f32[2,9]{1,0:T(2,128)} %gather_fusion.1, bf16[2,64,20,432]{3,2,1,0:T(8,128)(2,1)} %copy.49.picked_ref, bf16[96,20]{1,0:T(8,128)(2,1)} %constant.106.clone.spread_ref, bf16[96,432]{1,0:T(8,128)(2,1)} %constant.107.clone.mask_ref, bf16[2,64,48,128]{3,2,1,0:T(8,128)(2,1)} %bitcast.36, ...), custom_call_target="tpu_custom_call" | custom-call | flops 17213423616 | bytes 5357568 | tf_op jit(solution)/shard_map/pallas_call | solution.py:290
  159.0 0.8 copy.54
  159.9 0.1 multiply_reduce_fusion
  160.0 0.0 copy-done.3
  160.0 0.7 fusion.10
  (22 shorter events, 0.2 us)
Async XLA Ops:
  6.5 29.9 %copy-start = (f32[8,9]{1,0:T(8,128)S(1)}, f32[8,9]{1,0:T(8,128)}, u32[]{:S(2)}) copy-start(f32[8,9]{1,0:T(8,128)} %param.15) | copy-start | bytes 868
  6.5 0.8 copy-start.2
  6.5 2.3 %copy-start.4 = (s32[4,2]{0,1:T(2,128)S(1)}, s32[4,2]{0,1:T(2,128)}, u32[]{:S(2)}) copy-start(s32[4,2]{0,1:T(2,128)} %param.16) | copy-start | bytes 100
  6.5 2.5 %copy-start.5 = (bf16[2,128]{1,0:T(2,128)(2,1)S(1)}, bf16[2,128]{1,0:T(2,128)(2,1)}, u32[]{:S(2)}) copy-start(bf16[2,128]{1,0:T(2,128)(2,1)} %param.13) | copy-start | bytes 1540
  6.5 2.5 %copy-start.1 = (bf16[2,64,936]{2,1,0:T(8,128)(2,1)S(1)}, bf16[2,64,936]{2,1,0:T(8,128)(2,1)}, u32[]{:S(2)}) copy-start(bf16[2,64,936]{2,1,0:T(8,128)(2,1)} %table_ref.1) | copy-start | bytes 718852
  6.5 51.5 %all-gather.2.cloned.1.call-start = ((), (), s32[]{:S(2)}) async-start(), calls=%async_computation | async-start | bytes 7864320 | tf_op jit(solution)/shard_map/all_gather | solution.py:350
  7.3 32.9 %copy-start.6 = (s32[20,432]{1,0:T(8,128)S(1)}, s32[20,432]{1,0:T(8,128)}, u32[]{:S(2)}) copy-start(s32[20,432]{1,0:T(8,128)} %constant.105.clone) | copy-start | bytes 103684
  68.4 91.5 %copy-start.3 = (s32[2,512]{1,0:T(2,128)S(1)}, s32[2,512]{1,0:T(2,128)}, u32[]{:S(2)}) copy-start(s32[2,512]{1,0:T(2,128)} %param.18) | copy-start | bytes 12292
Sparse Core Ops, SparseCore 0:
  8.9 49.1 all-gather.1

commit v3 on v2

v3 whole, which is shorter than its diff:
```python
import functools

import jax
import jax.numpy as jnp
import numpy as np
from jax import lax
from jax.experimental import pallas as pl
from jax.experimental.pallas import tpu as pltpu
from jax.sharding import PartitionSpec as P

MODES = 9
CBANDS = 6
VBANDS = 4
BANDS = CBANDS * VBANDS
ROWS = MODES * 2 * BANDS

broadening = 0.1
MESH = pl.DeviceIdType.MESH


LANES = 128
ENTRIES = 16
CHUNKS = 4


def compact_index():
    index = np.full((CBANDS + VBANDS, LANES), -1, np.int32)
    lane = np.arange(2 * MODES * CBANDS)
    for d in range(CBANDS):
        index[d, : lane.size] = lane * CBANDS + d
    lane = np.arange(2 * MODES * VBANDS)
    for w in range(VBANDS):
        index[CBANDS + w, : lane.size] = 2 * MODES * CBANDS * CBANDS + lane * VBANDS + w
    return index


def compact_tables(table):
    index = compact_index()
    count, kpoints, size = table.shape
    select = (jnp.arange(size, dtype=jnp.int32)[:, None] == jnp.asarray(index).reshape(1, -1)).astype(table.dtype)
    rows = jnp.dot(table.reshape(count * kpoints, size), select).reshape(count, kpoints, index.shape[0], LANES)
    rows = jnp.pad(rows, ((0, 0), (0, 0), (0, ENTRIES - index.shape[0]), (0, 0)))
    return rows.reshape(count, kpoints * ENTRIES, LANES)


def lane_tables():
    u, pout, c, v = np.unravel_index(np.arange(ROWS), (MODES, 2, CBANDS, VBANDS))
    padded_rows = -(-ROWS // LANES) * LANES
    electron = np.zeros((LANES, 2, padded_rows), np.float32)
    hole = np.zeros((LANES, 2, padded_rows), np.float32)
    for pin in range(2):
        part = pout ^ pin
        electron[(part * MODES + u) * CBANDS + c, pin, np.arange(ROWS)] = 1
        hole[(part * MODES + u) * VBANDS + v, pin, np.arange(ROWS)] = 1
    return electron.reshape(LANES, -1), hole.reshape(LANES, -1)


def spread_tables():
    u, pout, c, v = np.unravel_index(np.arange(ROWS), (MODES, 2, CBANDS, VBANDS))
    spread = np.zeros((4 * BANDS, 2 * ENTRIES), np.float32)
    mask = np.zeros((4 * BANDS, -(-ROWS // LANES) * LANES), np.float32)
    row = 0
    for hole in range(2):
        for pin in range(2):
            sign = np.where((pout == 0) & (pin == 1), -1.0, 1.0)
            for band in range(CBANDS):
                for other in range(VBANDS):
                    spread[row, pin * ENTRIES + (CBANDS + other if hole else band)] = 1
                    mask[row, :ROWS] = -sign * (c == band) if hole else sign * (v == other)
                    row += 1
    return spread, mask


def greet(workers, parts):
    worker, part = lax.axis_index("wide"), lax.axis_index("narrow")
    barrier = pltpu.get_barrier_semaphore()
    me = worker * parts + part
    total = workers * parts

    def hello(step, carry):
        other = lax.rem(me + step, total)
        pl.semaphore_signal(
            barrier, inc=1, device_id={"wide": other // parts, "narrow": lax.rem(other, parts)}, device_id_type=MESH
        )
        return carry

    lax.fori_loop(1, total, hello, 0)
    pl.semaphore_wait(barrier, total - 1)


def to_all(workers, parts, source, landing, send_sem, recv_sem, wait):
    worker, part = lax.axis_index("wide"), lax.axis_index("narrow")
    me = worker * parts + part
    total = workers * parts

    def one(step, carry):
        other = lax.rem(me + step, total)
        copy = pltpu.make_async_remote_copy(
            src_ref=source,
            dst_ref=landing.at[me],
            send_sem=send_sem.at[step],
            recv_sem=recv_sem.at[step],
            device_id={"wide": other // parts, "narrow": lax.rem(other, parts)},
            device_id_type=MESH,
        )
        if wait:
            copy.wait()
        else:
            copy.start()
        return carry

    lax.fori_loop(1, total, one, 0)


def exchange_kernel(workers, parts, small_ref, small_out, smalls, s_send, s_recv):
    worker, part = lax.axis_index("wide"), lax.axis_index("narrow")
    greet(workers, parts)
    to_all(workers, parts, small_ref, smalls, s_send, s_recv, False)
    smalls[worker * parts + part] = small_ref[...]
    to_all(workers, parts, small_ref, smalls, s_send, s_recv, True)
    small_out[...] = smalls[...]


def exchange(workers, parts, small):
    total = workers * parts
    return pl.pallas_call(
        functools.partial(exchange_kernel, workers, parts),
        in_specs=[pl.BlockSpec(memory_space=pltpu.VMEM)],
        out_specs=pl.BlockSpec(memory_space=pltpu.VMEM),
        out_shape=jax.ShapeDtypeStruct((total,) + small.shape, small.dtype),
        scratch_shapes=[
            pltpu.VMEM((total,) + small.shape, small.dtype),
            pltpu.SemaphoreType.DMA((total,)),
            pltpu.SemaphoreType.DMA((total,)),
        ],
        compiler_params=pltpu.CompilerParams(collective_id=0, has_side_effects=True),
    )(small)


def rate_kernel(
    workers, parts, index_ref, omega_ref, table_ref, coeffs_ref, electron_ref, hole_ref, spread_ref, mask_ref,
    own_e_ref, far_e_ref, out_ref, *scratch,
):
    wholes, scratch = scratch[:CHUNKS], scratch[CHUNKS:]
    (
        tables, picked, near, staged, distant, mixed, rates, gathered, w_send, w_recv, f_send, f_recv,
        t_send, t_recv, tf_send, tf_recv, n_send, n_recv, m_send, m_recv, r_send, r_recv,
    ) = scratch
    worker, part = lax.axis_index("wide"), lax.axis_index("narrow")
    me = worker * parts + part
    half, chips = parts // 2, workers // 2
    chip, core = worker // 2, lax.rem(worker, 2)
    partner = chip * 2 + 1 - core
    side, place = part // half, lax.rem(part, half)
    share = index_ref.shape[0]
    owned, _, columns, trans = coeffs_ref.shape
    chunk = trans // CHUNKS
    width = half * columns
    count = table_ref.shape[0]
    table_half = table_ref.shape[1] // 2
    steps = chunk // (2 * BANDS)

    def remote(src, dst, send, recv, device):
        return pltpu.make_async_remote_copy(
            src_ref=src, dst_ref=dst, send_sem=send, recv_sem=recv, device_id=device, device_id_type=MESH
        )

    def block(c, owner):
        return wholes[c].at[pl.ds(owner * owned, owned)]

    def wide_copy(c, hop):
        source = coeffs_ref.at[:, :, :, pl.ds(c * chunk, chunk)]
        target = partner if hop == 0 else lax.rem(chip + hop, chips) * 2 + core
        return remote(source, block(c, worker), w_send.at[c, hop], w_recv.at[c, hop], {"wide": target})

    def arrived(hop):
        return partner if hop == 0 else lax.rem(chip - hop + chips, chips) * 2 + core

    def wide_wait(c, hop):
        landing = block(c, arrived(hop))
        return remote(landing, landing, w_send.at[c, hop], w_recv.at[c, hop], {"wide": partner})

    def forward(c, hop):
        landing = block(c, arrived(hop))
        return remote(landing, landing, f_send.at[c, hop], f_recv.at[c, hop], {"wide": partner})

    def forward_wait(c, hop):
        landing = block(c, lax.rem(chip - hop + chips, chips) * 2 + 1 - core)
        return remote(landing, landing, f_send.at[c, hop], f_recv.at[c, hop], {"wide": partner})

    def table_rows(owner, which):
        start = pl.multiple_of(which * table_half, table_half)
        return tables.at[pl.ds(owner * count, count), pl.ds(start, table_half)]

    def table_copy(step):
        start = pl.multiple_of(core * table_half, table_half)
        return remote(
            table_ref.at[:, pl.ds(start, table_half)], table_rows(part, core), t_send.at[step], t_recv.at[step],
            {"narrow": lax.rem(part + step, parts)},
        )

    def table_arrival(step, which, send, recv):
        landing = table_rows(lax.rem(part - step + parts, parts), which)
        return remote(landing, landing, send.at[step], recv.at[step], {"wide": partner})

    def rows_of(c):
        return pl.ds(c * chunk, chunk)

    def near_copy(pair, c, i):
        ref = near.at[pair, place, :, rows_of(c)]
        return remote(ref, ref, n_send.at[pair, c, i], n_recv.at[pair, c, place], {"narrow": side * half + i})

    def near_wait(pair, c, i):
        ref = near.at[pair, i, :, rows_of(c)]
        return remote(ref, ref, n_send.at[pair, c, i], n_recv.at[pair, c, i], {"narrow": side * half + i})

    def far_copy(pair, c, t):
        slot = lax.rem(part, 2)
        return remote(
            staged.at[pair, :, :, rows_of(c)], distant.at[pair, slot, :, :, rows_of(c)],
            m_send.at[pair, c, t], m_recv.at[pair, c, slot], {"narrow": t * half + part // 2},
        )

    def far_wait(pair, c, s):
        ref = distant.at[pair, s, :, :, rows_of(c)]
        return remote(ref, ref, m_send.at[pair, c, s], m_recv.at[pair, c, s], {"narrow": place * 2 + s})

    def stage_near(pair, c):
        rows = wholes[c][index_ref[pair, 0]]
        for p in range(2):
            near[pair, place, p, rows_of(c)] = rows[p].T
        for i in range(half):
            pl.when(side * half + i != part)(near_copy(pair, c, i).start)

    def stage_far(pair, c):
        rows = wholes[c][index_ref[pair, 1]]
        staged[pair, :, :, rows_of(c)] = rows
        for t in range(2):
            target = t * half + part // 2
            pl.when(target != part)(far_copy(pair, c, t).start)

            @pl.when(target == part)
            def _():
                distant[pair, lax.rem(part, 2), :, :, rows_of(c)] = rows

    def pick(pair):
        size = 256
        lanes = 2 * mask_ref.shape[1]

        def some(step, carry):
            rows = pl.ds(pl.multiple_of(step * size, size), size)
            entries = tables[index_ref[pair, 2], rows]
            electron = jnp.dot(entries, electron_ref[...], preferred_element_type=jnp.float32)
            hole = jnp.dot(entries, hole_ref[...], preferred_element_type=jnp.float32)
            entry = lax.rem(lax.broadcasted_iota(jnp.int32, (size, lanes), 0), ENTRIES)
            picked[pair, rows] = jnp.where(entry < CBANDS, electron, hole).astype(jnp.bfloat16)
            return carry

        lax.fori_loop(0, table_ref.shape[1] // size, some, 0)

    def mix(pair, c):
        for i in range(half):
            pl.when(side * half + i != part)(near_wait(pair, c, i).wait_recv)
        lanes = mask_ref.shape[1]

        def some(step, carry):
            start = pl.multiple_of(step * 2 * BANDS, 2 * BANDS)
            whole_rows = [
                jnp.concatenate([near[pair, i, p, pl.ds(start, 2 * BANDS)] for i in range(half)], axis=1).astype(
                    jnp.float32
                )
                for p in range(2)
            ]
            blocks = []
            for offset in range(2):
                first = pl.multiple_of((step * 2 + offset) * ENTRIES, ENTRIES)
                entries = picked[pair, pl.ds(first, ENTRIES)]
                entries = jnp.concatenate([entries[:, :lanes], entries[:, lanes:]], axis=0)
                spread = jnp.dot(spread_ref[...], entries, preferred_element_type=jnp.float32)
                gain = (spread.astype(jnp.bfloat16) * mask_ref[...])[:, :ROWS]
                rows = jnp.concatenate([part_rows[offset * BANDS : (offset + 1) * BANDS] for part_rows in whole_rows], axis=0)
                rows = rows.astype(jnp.bfloat16)
                rows = jnp.concatenate([rows, rows], axis=0)
                blocks.append(
                    lax.dot_general(gain, rows, (((0,), (0,)), ((), ())), preferred_element_type=jnp.float32)
                )
            for u in range(MODES):
                for p in range(2):
                    low = (u * 2 + p) * BANDS
                    both = jnp.concatenate([one[low : low + BANDS] for one in blocks], axis=0)
                    mixed[u, pl.ds(start, 2 * BANDS), p * width : (p + 1) * width] = both.astype(jnp.bfloat16)
            return carry

        lax.fori_loop(c * steps, (c + 1) * steps, some, 0)

    def couple(pair):
        for c in range(CHUNKS):
            for s in range(2):
                pl.when(place * 2 + s != part)(far_wait(pair, c, s).wait_recv)
        far_rows = distant[pair].reshape(4 * columns, trans)
        gap = far_e_ref[pair] - own_e_ref[pair]

        def mode(u, total):
            coupled = jnp.dot(far_rows, mixed[u], preferred_element_type=jnp.float32)
            coupled = coupled.reshape(2, 2, columns, 2 * width)
            real = coupled[:, 0, :, :width] + coupled[:, 1, :, width:]
            imag = coupled[:, 0, :, width:] - coupled[:, 1, :, :width]
            scaled = (gap - omega_ref[pair, u]) / broadening
            power = (real * real + imag * imag).reshape(2 * columns, width) / (1.0 + scaled * scaled)
            return total + jnp.sum(power, axis=0, keepdims=True)

        rates[pair] = lax.fori_loop(0, MODES, mode, jnp.zeros((1, width), jnp.float32))

    greet(workers, parts)
    for c in range(CHUNKS):
        for hop in range(chips):
            wide_copy(c, hop).start()
    for step in range(1, parts):
        table_copy(step).start()
    for c in range(CHUNKS):
        wholes[c][pl.ds(worker * owned, owned)] = coeffs_ref[:, :, :, rows_of(c)]
    tables[pl.ds(part * count, count)] = table_ref[...]

    for c in range(CHUNKS):
        for hop in range(1, chips):
            wide_wait(c, hop).wait_recv()
            forward(c, hop).start()
        wide_wait(c, 0).wait_recv()
        for hop in range(1, chips):
            forward_wait(c, hop).wait_recv()
        stage_near(0, c)
        stage_far(0, c)
        if c == 0:
            for step in range(1, parts):
                table_arrival(step, core, t_send, t_recv).wait_recv()
                table_arrival(step, core, tf_send, tf_recv).start()
        if c == 1:
            for step in range(1, parts):
                table_arrival(step, 1 - core, tf_send, tf_recv).wait_recv()
            for pair in range(share):
                pick(pair)
        if c == 2:
            mix(0, 0)
    for pair in range(1, share):
        for c in range(CHUNKS):
            stage_near(pair, c)
        for c in range(CHUNKS):
            stage_far(pair, c)
    for c in range(1, CHUNKS):
        mix(0, c)
    couple(0)
    for pair in range(1, share):
        for c in range(CHUNKS):
            mix(pair, c)
        couple(pair)

    gathered[me] = rates[...]
    to_all(workers, parts, rates, gathered, r_send, r_recv, False)
    for c in range(CHUNKS):
        for hop in range(chips):
            wide_copy(c, hop).wait_send()
            if hop:
                forward(c, hop).wait_send()
        for pair in range(share):
            for i in range(half):
                pl.when(side * half + i != part)(near_copy(pair, c, i).wait_send)
            for t in range(2):
                pl.when(t * half + part // 2 != part)(far_copy(pair, c, t).wait_send)
    for step in range(1, parts):
        table_copy(step).wait_send()
        table_arrival(step, core, tf_send, tf_recv).wait_send()
    to_all(workers, parts, rates, gathered, r_send, r_recv, True)
    out_ref[...] = gathered[...]


def pair_rates(workers, parts, index, omega, table, coeffs, own_e, far_e):
    share = index.shape[0]
    owned, _, columns, trans = coeffs.shape
    total, half, chips = workers * parts, parts // 2, workers // 2
    width = half * columns
    electron, hole = lane_tables()
    spread, mask = spread_tables()
    constants = [jnp.asarray(one, jnp.bfloat16) for one in (electron, hole, spread, mask)]
    flops = 2 * share * (trans // BANDS * 4 * BANDS * ROWS * width + 8 * columns * trans * MODES * width)
    smem, vmem = pl.BlockSpec(memory_space=pltpu.SMEM), pl.BlockSpec(memory_space=pltpu.VMEM)
    dma, bf16 = pltpu.SemaphoreType.DMA, jnp.bfloat16
    return pl.pallas_call(
        functools.partial(rate_kernel, workers, parts),
        in_specs=[smem, smem] + [vmem] * 8,
        out_specs=vmem,
        out_shape=jax.ShapeDtypeStruct((total, share, 1, width), jnp.float32),
        scratch_shapes=[pltpu.VMEM((owned * workers, 2, columns, trans // CHUNKS), bf16)] * CHUNKS
        + [
            pltpu.VMEM((table.shape[0] * parts,) + table.shape[1:], bf16),
            pltpu.VMEM((share, table.shape[1], electron.shape[1]), bf16),
            pltpu.VMEM((share, half, 2, trans, columns), bf16),
            pltpu.VMEM((share, 2, columns, trans), bf16),
            pltpu.VMEM((share, 2, 2, columns, trans), bf16),
            pltpu.VMEM((MODES, trans, 2 * width), bf16),
            pltpu.VMEM((share, 1, width), jnp.float32),
            pltpu.VMEM((total, share, 1, width), jnp.float32),
        ]
        + [dma((CHUNKS, chips))] * 4
        + [dma((parts,))] * 4
        + [dma((share, CHUNKS, half))] * 2
        + [dma((share, CHUNKS, 2))] * 2
        + [dma((total,))] * 2,
        compiler_params=pltpu.CompilerParams(
            collective_id=1, has_side_effects=True, vmem_limit_bytes=60 * 1024 * 1024
        ),
        cost_estimate=pl.CostEstimate(flops=flops, bytes_accessed=4 * coeffs.size, transcendentals=0),
    )(index, omega, table, coeffs, *constants, own_e, far_e)


def shards(coeffs, energies, g_coupling, omega, pairs, counts, blocks):
    worker = lax.axis_index("wide")
    part = lax.axis_index("narrow")
    workers = lax.axis_size("wide")
    owned, _, columns, trans = coeffs.shape
    momenta = owned * workers
    slots = pairs.shape[0]
    excitons = blocks.shape[1]

    parts = lax.axis_size("narrow")
    small = jnp.concatenate([energies.astype(jnp.float32).reshape(-1), pairs.astype(jnp.float32).reshape(-1)])
    small = jnp.pad(small, (0, -small.shape[0] % 128)).reshape(1, -1)
    small = exchange(workers, parts, small)
    small = small.reshape(workers, parts, small.shape[-1])
    levels = small[:, :, : owned * columns].reshape(workers, -1, owned, columns)
    levels = levels.transpose(0, 2, 1, 3).reshape(momenta, excitons)
    all_pairs = small[:, 0, owned * columns : owned * columns + 2 * slots].astype(jnp.int32).reshape(workers * slots, 2)

    ends = jnp.sum(jnp.where(jnp.arange(workers)[:, None] <= jnp.arange(workers)[None, :], counts[:, None], 0), axis=0)
    live = jnp.arange(momenta)
    holder = jnp.sum((ends[None, :] <= live[:, None]).astype(jnp.int32), axis=1)
    holder = jnp.minimum(holder, workers - 1)
    slot = holder * slots + live - (jnp.take(ends, holder) - jnp.take(counts, holder))
    live_pairs = jnp.take(all_pairs, jnp.clip(slot, 0, workers * slots - 1), axis=0)
    live_home = live_pairs[:, 0]
    mine = lax.dynamic_slice_in_dim(live_pairs, worker * owned, owned, 0)
    home, shift = mine[:, 0], mine[:, 1]
    far_index = (home + shift) % momenta

    frequency = jnp.take(omega, shift, axis=0, mode="clip")
    index = jnp.stack([home, far_index, shift], axis=1)

    half = parts // 2
    own_e = jnp.take(levels, home, axis=0, mode="clip")
    own_e = lax.dynamic_slice_in_dim(own_e, part // half * half * columns, half * columns, 1)
    far_e = jnp.take(levels, far_index, axis=0, mode="clip")
    far_e = lax.dynamic_slice_in_dim(far_e, part % half * 2 * columns, 2 * columns, 1)
    rates = pair_rates(
        workers, parts, index, frequency, compact_tables(g_coupling), coeffs, own_e[:, None, :], far_e[:, :, None]
    )

    rates = rates.reshape(workers, 2, half, owned, half * columns).sum(axis=2)
    rates = rates.transpose(0, 2, 1, 3).reshape(momenta, excitons)
    local = worker * owned + jnp.arange(owned)
    chosen = (live_home[None, :] == local[:, None]).astype(jnp.float32)
    total = jnp.sum(chosen[:, :, None] * rates[None, :, :], axis=1)
    margin = 3
    widened = jnp.pad(total, ((0, 0), (margin, margin)))
    padded_labels = jnp.pad(blocks, ((0, 0), (margin, margin)), constant_values=-1)
    widened = lax.dynamic_slice_in_dim(widened, part * columns, columns + 2 * margin, 1)
    near_labels = lax.dynamic_slice_in_dim(padded_labels, part * columns, columns + 2 * margin, 1)
    my_labels = near_labels[:, margin : margin + columns]
    upper = jnp.zeros((owned, columns), jnp.float32)
    lower = jnp.zeros((owned, columns), jnp.float32)
    for offset in range(2 * margin + 1):
        same = (near_labels[:, offset : offset + columns] == my_labels).astype(jnp.float32)
        upper += same * widened[:, offset : offset + columns]
        lower += same
    return upper / lower


def solution(mesh):
    in_specs = (
        P(("groups", "wide"), None, "narrow", None),
        P(("groups", "wide"), "narrow"),
        P(("groups", "narrow"), None, None),
        P("groups", None),
        P(("groups", "wide"), None),
        P("groups"),
        P(("groups", "wide"), None),
    )
    out_specs = P(("groups", "wide"), "narrow")
    return jax.shard_map(shards, mesh=mesh, in_specs=in_specs, out_specs=out_specs, check_vma=False)
```

time: 168 us -> 139 us (0.83)
  between operations: 13.7 us -> 0.18 us
  local copies, waits for them, and re-layouts: 20.9 us -> 9.91 us
  waiting for transfers between devices: 7.25 us -> 0 us
  matrix products: 7.92 us -> 1.65 us
  Pallas kernels: 116 us -> 122 us
  other arithmetic: 1.46 us -> 4.9 us
    pallas_call x1, Pallas kernels: 90.6 us -> 112 us  [pair_rates(): pl.pallas_call(functools.partial(rate_kernel, workers, parts), in_specs=[...]
    pallas_call x1, Pallas kernels: 25.7 us -> 9.9 us  [exchange(): pl.pallas_call(functools.partial(exchange_kernel, workers, parts), in_spe...]
    gather x4 -> x0, local copies, waits for them, and re-layouts: 9.46 us -> none  [the longest x1 4.56 us: shards(): far = jnp.take(whole, far_index, axis=0, mode='clip')]
    dot_general x1 -> x0, matrix products: 7.92 us -> none  [pick_coupling(): picked = jnp.dot(chosen.reshape(share * kpoints, width), select)]
    all_gather x1 -> x0, waiting for transfers between devices: 6.57 us -> none  [shards(): whole = lax.all_gather(coeffs, 'wide', axis=0, tiled=True)]
    dot_general x1, local copies, waits for them, and re-layouts: 3.21 us -> 0.18 us  [compact_tables(): jnp.dot(table.reshape(count * kpoints, size), select)]
  transfers between devices with their start and end apart: 1 -> 0, of which waited for: 1 -> 0; matrix products, arithmetic and copies ran while one was open for 11% -> 0% of each run, Pallas kernels for 15% -> 0%
where the time goes in v3:
time: 139 us; the launch traced here: 138 us
  Pallas kernels  122 us (88%)
  local copies, waits for them, and re-layouts  9.91 us (7%)
  other arithmetic  4.9 us (4%)
  matrix products  1.65 us (1%)
    pallas_call x1, Pallas kernels, pair_rates(): pl.pallas_call(functools.partial(rate_kernel, workers, parts), in_specs=[...  112 us
    pallas_call x1, Pallas kernels, exchange(): pl.pallas_call(functools.partial(exchange_kernel, workers, parts), in_spe...  9.9 us

profile of v3, /device:TPU:0, one launch (start us, length us, event | category | flops | bytes accessed | tf_op | source)
XLA Modules:
  0.0 138.4 jit_solution(10097861631424352198)
XLA Ops:
  0.0 0.0 copy-start
  0.0 0.7 convert_element_type.49
  0.7 0.1 copy.33
  0.8 0.1 reshape.86
  0.9 0.7 bitcast_convert_fusion
  1.6 0.6 reshape.87.small_ref
  2.1 9.9 %shard_map.118 = f32[16,1,384]{2,1,0:T(1,128)} custom-call(f32[1,384]{1,0:T(1,128)} %reshape.87.small_ref), custom_call_target="tpu_custom_call" | custom-call | tf_op jit(solution)/shard_map/pallas_call | solution.py:126
  12.0 0.8 reduce
  12.9 0.1 convert_element_type.51
  13.0 0.7 select_reduce_fusion
  13.7 0.1 convert_reduce_fusion
  13.8 1.3 gather_fusion.5
  15.1 0.6 gather_fusion.4
  15.8 0.6 gather_fusion
  16.4 0.1 broadcast_select_fusion
  16.4 0.2 slice_reduce_fusion.2
  16.7 0.6 pad_add_fusion.index_ref
  17.3 1.8 %gather_fusion.1 = f32[2,9]{1,0:T(2,128)} fusion(f32[8,9]{1,0:T(8,128)} %param.17, s32[1024]{0:T(1024)S(1)} %pad_clamp_fusion.2), kind=kCustom, calls=%fused_computation.3 | custom fusion | bytes 152 | tf_op jit(solution)/shard_map/jit(_take)/gather | solution.py:444
  19.1 0.0 copy-done
  19.1 1.6 %fusion.3 = bf16[128,1280]{0,1:T(8,128)(2,1)S(1)} fusion(bf16[128,936]{1,0:T(8,128)(2,1)S(1)} %bitcast.26, s32[1280]{0:T(1024)} %constant.129), kind=kOutput, calls=%fused_computation.10 | convolution fusion | flops 309268480 | bytes 572416
  20.8 0.2 copy.35
  21.0 0.2 reshape.90
  21.2 0.9 pad.18
  22.1 0.6 gather_fusion.2
  22.7 0.6 broadcast_in_dim.46.own_e_ref
  23.2 0.6 gather_fusion.3
  23.8 0.9 copy.37.far_e_ref
  24.7 0.0 copy-start.1
  24.7 111.9 %shard_map.119 = f32[16,2,1,256]{3,2,1,0:T(1,128)} custom-call(s32[2,3]{1,0:T(2,128)} %pad_add_fusion.index_ref, f32[2,9]{1,0:T(2,128)} %gather_fusion.1, bf16[2,1024,128]{2,1,0:T(8,128)(2,1)} %bitcast.27, bf16[2,2,128,1536]{3,2,1,0:T(8,128)(2,1)} %coeffs_ref.1, bf16[128,1024]{1,0:T(8,128)(2,1)} %constant.112.clone.electron_ref, ...), custom_call_target="tpu_custom_call" | custom-call | flops 17213423616 | bytes 3145728 | tf_op jit(solution)/shard_map/pallas_call | solution.py:387
  136.6 0.8 copy.40
  137.4 0.1 slice_reduce_fusion
  137.5 0.1 compare_convert_fusion
  137.6 0.1 multiply_reduce_fusion
  137.7 0.0 copy-done.1
  137.7 0.7 fusion.11
  (19 shorter events, 0.2 us)
Async XLA Ops:
  0.0 19.1 %copy-start = (bf16[2,64,936]{2,1,0:T(8,128)(2,1)S(1)}, bf16[2,64,936]{2,1,0:T(8,128)(2,1)}, u32[]{:S(2)}) copy-start(bf16[2,64,936]{2,1,0:T(8,128)(2,1)} %param.16) | copy-start | bytes 718852
  24.7 113.0 %copy-start.1 = (s32[2,512]{1,0:T(2,128)S(1)}, s32[2,512]{1,0:T(2,128)}, u32[]{:S(2)}) copy-start(s32[2,512]{1,0:T(2,128)} %param.20) | copy-start | bytes 12292

commit v4 on v3

--- a/solution.py
+++ b/solution.py
@@ -39,8 +39,15 @@
     count, kpoints, size = table.shape
     select = (jnp.arange(size, dtype=jnp.int32)[:, None] == jnp.asarray(index).reshape(1, -1)).astype(table.dtype)
     rows = jnp.dot(table.reshape(count * kpoints, size), select).reshape(count, kpoints, index.shape[0], LANES)
-    rows = jnp.pad(rows, ((0, 0), (0, 0), (0, ENTRIES - index.shape[0]), (0, 0)))
-    return rows.reshape(count, kpoints * ENTRIES, LANES)
+    return rows.reshape(count, kpoints * index.shape[0], LANES)
+
+
+def pad_table():
+    row = np.arange(ENTRIES * ENTRIES)
+    kept = row % ENTRIES < CBANDS + VBANDS
+    pad = np.zeros((row.size, ENTRIES * (CBANDS + VBANDS)), np.float32)
+    pad[row[kept], (row // ENTRIES * (CBANDS + VBANDS) + row % ENTRIES)[kept]] = 1
+    return pad
 
 
 def lane_tables():
@@ -138,12 +145,12 @@
 
 
 def rate_kernel(
-    workers, parts, index_ref, omega_ref, table_ref, coeffs_ref, electron_ref, hole_ref, spread_ref, mask_ref,
-    own_e_ref, far_e_ref, out_ref, *scratch,
+    workers, parts, index_ref, omega_ref, table_ref, coeffs_ref, pad_ref, electron_ref, hole_ref, spread_ref,
+    mask_ref, small_ref, out_ref, *scratch,
 ):
     wholes, scratch = scratch[:CHUNKS], scratch[CHUNKS:]
     (
-        tables, picked, near, staged, distant, mixed, rates, gathered, w_send, w_recv, f_send, f_recv,
+        tables, picked, near, staged, distant, mixed, partial, rates, gathered, w_send, w_recv, f_send, f_recv,
         t_send, t_recv, tf_send, tf_recv, n_send, n_recv, m_send, m_recv, r_send, r_recv,
     ) = scratch
     worker, part = lax.axis_index("wide"), lax.axis_index("narrow")
@@ -244,19 +251,20 @@
                 distant[pair, lax.rem(part, 2), :, :, rows_of(c)] = rows
 
     def pick(pair):
-        size = 256
+        size, kept = pad_ref.shape
         lanes = 2 * mask_ref.shape[1]
 
         def some(step, carry):
             rows = pl.ds(pl.multiple_of(step * size, size), size)
-            entries = tables[index_ref[pair, 2], rows]
+            packed = tables[index_ref[pair, 2], pl.ds(pl.multiple_of(step * kept, kept), kept)]
+            entries = jnp.dot(pad_ref[...], packed, preferred_element_type=jnp.float32).astype(jnp.bfloat16)
             electron = jnp.dot(entries, electron_ref[...], preferred_element_type=jnp.float32)
             hole = jnp.dot(entries, hole_ref[...], preferred_element_type=jnp.float32)
             entry = lax.rem(lax.broadcasted_iota(jnp.int32, (size, lanes), 0), ENTRIES)
             picked[pair, rows] = jnp.where(entry < CBANDS, electron, hole).astype(jnp.bfloat16)
             return carry
 
-        lax.fori_loop(0, table_ref.shape[1] // size, some, 0)
+        lax.fori_loop(0, table_ref.shape[1] // kept, some, 0)
 
     def mix(pair, c):
         for i in range(half):
@@ -293,23 +301,48 @@
 
         lax.fori_loop(c * steps, (c + 1) * steps, some, 0)
 
-    def couple(pair):
-        for c in range(CHUNKS):
+    def gap_of(pair):
+        own = [small_ref[index_ref[pair, 3] + side * half + i, pl.ds(index_ref[pair, 4], 1)] for i in range(half)]
+        own = jnp.concatenate(own, axis=1)
+        far = []
+        for s in range(2):
+            row = small_ref[index_ref[pair, 5] + place * 2 + s, pl.ds(index_ref[pair, 6], 1)]
+            column = jnp.broadcast_to(row, (columns, columns)).T
+            far.append(jnp.concatenate([column] * half, axis=1))
+        return jnp.concatenate(far, axis=0) - own
+
+    def far_arrival(pair, first, last):
+        for c in range(first, last):
             for s in range(2):
                 pl.when(place * 2 + s != part)(far_wait(pair, c, s).wait_recv)
-        far_rows = distant[pair].reshape(4 * columns, trans)
-        gap = far_e_ref[pair] - own_e_ref[pair]
-
-        def mode(u, total):
-            coupled = jnp.dot(far_rows, mixed[u], preferred_element_type=jnp.float32)
-            coupled = coupled.reshape(2, 2, columns, 2 * width)
-            real = coupled[:, 0, :, :width] + coupled[:, 1, :, width:]
-            imag = coupled[:, 0, :, width:] - coupled[:, 1, :, :width]
-            scaled = (gap - omega_ref[pair, u]) / broadening
-            power = (real * real + imag * imag).reshape(2 * columns, width) / (1.0 + scaled * scaled)
-            return total + jnp.sum(power, axis=0, keepdims=True)
-
-        rates[pair] = lax.fori_loop(0, MODES, mode, jnp.zeros((1, width), jnp.float32))
+
+    def weigh(pair, u, coupled, gap):
+        coupled = coupled.reshape(2, 2, columns, 2 * width)
+        real = coupled[:, 0, :, :width] + coupled[:, 1, :, width:]
+        imag = coupled[:, 0, :, width:] - coupled[:, 1, :, :width]
+        scaled = (gap - omega_ref[index_ref[pair, 2], u]) / broadening
+        power = (real * real + imag * imag).reshape(2 * columns, width) / (1.0 + scaled * scaled)
+        return jnp.sum(power, axis=0, keepdims=True)
+
+    def couple(pair):
+        cut = trans // 2
+        gap = gap_of(pair)
+        far_arrival(pair, 0, CHUNKS // 2)
+
+        def start(u, carry):
+            far_rows = distant[pair, :, :, :, :cut].reshape(4 * columns, cut)
+            partial[u] = jnp.dot(far_rows, mixed[u, :cut], preferred_element_type=jnp.float32)
+            return carry
+
+        lax.fori_loop(0, MODES, start, 0)
+        far_arrival(pair, CHUNKS // 2, CHUNKS)
+
+        def finish(u, total):
+            far_rows = distant[pair, :, :, :, cut:].reshape(4 * columns, trans - cut)
+            coupled = partial[u] + jnp.dot(far_rows, mixed[u, cut:], preferred_element_type=jnp.float32)
+            return total + weigh(pair, u, coupled, gap)
+
+        rates[pair] = lax.fori_loop(0, MODES, finish, jnp.zeros((1, width), jnp.float32))
 
     greet(workers, parts)
     for c in range(CHUNKS):
@@ -373,14 +406,14 @@
     out_ref[...] = gathered[...]
 
 
-def pair_rates(workers, parts, index, omega, table, coeffs, own_e, far_e):
+def pair_rates(workers, parts, index, omega, table, coeffs, small):
     share = index.shape[0]
     owned, _, columns, trans = coeffs.shape
     total, half, chips = workers * parts, parts // 2, workers // 2
     width = half * columns
     electron, hole = lane_tables()
     spread, mask = spread_tables()
-    constants = [jnp.asarray(one, jnp.bfloat16) for one in (electron, hole, spread, mask)]
+    constants = [jnp.asarray(one, jnp.bfloat16) for one in (pad_table(), electron, hole, spread, mask)]
     flops = 2 * share * (trans // BANDS * 4 * BANDS * ROWS * width + 8 * columns * trans * MODES * width)
     smem, vmem = pl.BlockSpec(memory_space=pltpu.SMEM), pl.BlockSpec(memory_space=pltpu.VMEM)
     dma, bf16 = pltpu.SemaphoreType.DMA, jnp.bfloat16
@@ -392,11 +425,12 @@
         scratch_shapes=[pltpu.VMEM((owned * workers, 2, columns, trans // CHUNKS), bf16)] * CHUNKS
         + [
             pltpu.VMEM((table.shape[0] * parts,) + table.shape[1:], bf16),
-            pltpu.VMEM((share, table.shape[1], electron.shape[1]), bf16),
+            pltpu.VMEM((share, trans // BANDS * ENTRIES, electron.shape[1]), bf16),
             pltpu.VMEM((share, half, 2, trans, columns), bf16),
             pltpu.VMEM((share, 2, columns, trans), bf16),
             pltpu.VMEM((share, 2, 2, columns, trans), bf16),
             pltpu.VMEM((MODES, trans, 2 * width), bf16),
+            pltpu.VMEM((MODES, 4 * columns, 2 * width), jnp.float32),
             pltpu.VMEM((share, 1, width), jnp.float32),
             pltpu.VMEM((total, share, 1, width), jnp.float32),
         ]
@@ -409,7 +443,7 @@
             collective_id=1, has_side_effects=True, vmem_limit_bytes=60 * 1024 * 1024
         ),
         cost_estimate=pl.CostEstimate(flops=flops, bytes_accessed=4 * coeffs.size, transcendentals=0),
-    )(index, omega, table, coeffs, *constants, own_e, far_e)
+    )(index, omega, table, coeffs, *constants, small)
 
 
 def shards(coeffs, energies, g_coupling, omega, pairs, counts, blocks):
@@ -422,37 +456,33 @@
     excitons = blocks.shape[1]
 
     parts = lax.axis_size("narrow")
-    small = jnp.concatenate([energies.astype(jnp.float32).reshape(-1), pairs.astype(jnp.float32).reshape(-1)])
-    small = jnp.pad(small, (0, -small.shape[0] % 128)).reshape(1, -1)
-    small = exchange(workers, parts, small)
-    small = small.reshape(workers, parts, small.shape[-1])
-    levels = small[:, :, : owned * columns].reshape(workers, -1, owned, columns)
-    levels = levels.transpose(0, 2, 1, 3).reshape(momenta, excitons)
-    all_pairs = small[:, 0, owned * columns : owned * columns + 2 * slots].astype(jnp.int32).reshape(workers * slots, 2)
-
-    ends = jnp.sum(jnp.where(jnp.arange(workers)[:, None] <= jnp.arange(workers)[None, :], counts[:, None], 0), axis=0)
-    live = jnp.arange(momenta)
-    holder = jnp.sum((ends[None, :] <= live[:, None]).astype(jnp.int32), axis=1)
-    holder = jnp.minimum(holder, workers - 1)
-    slot = holder * slots + live - (jnp.take(ends, holder) - jnp.take(counts, holder))
-    live_pairs = jnp.take(all_pairs, jnp.clip(slot, 0, workers * slots - 1), axis=0)
-    live_home = live_pairs[:, 0]
-    mine = lax.dynamic_slice_in_dim(live_pairs, worker * owned, owned, 0)
+    listed = jnp.pad(pairs.astype(jnp.float32).reshape(1, -1), ((0, 0), (0, columns - 2 * slots)))
+    small = exchange(workers, parts, jnp.concatenate([energies.astype(jnp.float32), listed], axis=0))
+    listed = small.reshape(workers, parts, owned + 1, columns)[:, 0, owned, : 2 * slots]
+    listed = listed.reshape(workers, slots, 2)
+
+    before = jnp.arange(workers)[:, None] > jnp.arange(workers)[None, :]
+    rank = jnp.sum(jnp.where(before, counts[None, :], 0), axis=1)[:, None] + jnp.arange(slots)[None, :]
+    rank = jnp.where(jnp.arange(slots)[None, :] < counts[:, None], rank, -1)
+
+    def live_rows(wanted):
+        hit = (rank[None, :, :] == wanted[:, None, None])[..., None]
+        return jnp.sum(jnp.where(hit, listed[None], 0.0), axis=(1, 2)).astype(jnp.int32)
+
+    mine = live_rows(worker * owned + jnp.arange(owned))
     home, shift = mine[:, 0], mine[:, 1]
     far_index = (home + shift) % momenta
-
-    frequency = jnp.take(omega, shift, axis=0, mode="clip")
-    index = jnp.stack([home, far_index, shift], axis=1)
-
+    index = jnp.stack(
+        [
+            home, far_index, shift,
+            home // owned * parts, home % owned, far_index // owned * parts, far_index % owned,
+        ],
+        axis=1,
+    )
+    rates = pair_rates(workers, parts, index, omega, compact_tables(g_coupling), coeffs, small)
+
+    live_home = live_rows(jnp.arange(momenta))[:, 0]
     half = parts // 2
-    own_e = jnp.take(levels, home, axis=0, mode="clip")
-    own_e = lax.dynamic_slice_in_dim(own_e, part // half * half * columns, half * columns, 1)
-    far_e = jnp.take(levels, far_index, axis=0, mode="clip")
-    far_e = lax.dynamic_slice_in_dim(far_e, part % half * 2 * columns, 2 * columns, 1)
-    rates = pair_rates(
-        workers, parts, index, frequency, compact_tables(g_coupling), coeffs, own_e[:, None, :], far_e[:, :, None]
-    )
-
     rates = rates.reshape(workers, 2, half, owned, half * columns).sum(axis=2)
     rates = rates.transpose(0, 2, 1, 3).reshape(momenta, excitons)
     local = worker * owned + jnp.arange(owned)

time: 139 us -> 122 us (0.88)
  Pallas kernels: 122 us -> 110 us
  local copies, waits for them, and re-layouts: 9.91 us -> 4.85 us
    pallas_call x1, Pallas kernels: 112 us -> 101 us  [pair_rates(): pl.pallas_call(functools.partial(rate_kernel, workers, parts), in_specs=[...]
    gather x6 -> x0, local copies, waits for them, and re-layouts: 5.43 us -> none  [the longest x1 1.81 us: shards(): frequency = jnp.take(omega, shift, axis=0, mode='clip')]
    another operation x0 -> x2, local copies, waits for them, and re-layouts: none -> 1.76 us  [the longest x1 1.11 us: compact_tables(): return rows.reshape(count, kpoints * index.shape[0], LANES)]
where the time goes in v4:
time: 122 us
  Pallas kernels  110 us (90%)
  local copies, waits for them, and re-layouts  4.85 us (4%)
  other arithmetic  4.79 us (4%)
  matrix products  1.65 us (1%)
    pallas_call x1, Pallas kernels, pair_rates(): pl.pallas_call(functools.partial(rate_kernel, workers, parts), in_specs=[...  101 us
    pallas_call x1, Pallas kernels, exchange(): pl.pallas_call(functools.partial(exchange_kernel, workers, parts), in_spe...  9.94 us

profile of v4, /device:TPU:0, one launch (start us, length us, event | category | flops | bytes accessed | tf_op | source)
XLA Modules:
  0.0 121.8 jit_solution(637652621724281176)
XLA Ops:
  0.0 0.0 copy-start
  0.0 0.9 copy-done
  1.0 0.8 select_reduce_fusion.2
  1.7 0.7 convert_element_type.44
  2.4 0.7 convert_element_type.45
  3.1 0.1 copy.35
  3.2 0.1 reshape.95
  3.2 0.6 select_maximum_fusion.small_ref
  3.9 0.7 add_select_fusion
  4.6 0.1 broadcast_compare_fusion
  4.7 0.1 iota_compare_fusion.1
  4.7 9.9 %shard_map.127.small_ref = f32[16,3,128]{2,1,0:T(4,128)} custom-call(f32[3,128]{1,0:T(4,128)} %select_maximum_fusion.small_ref), custom_call_target="tpu_custom_call" | custom-call | tf_op jit(solution)/shard_map/pallas_call | solution.py:133
  14.7 0.7 slice.73
  15.4 0.1 copy.42
  15.5 0.1 copy.38
  15.6 0.1 select_reduce_fusion.1
  15.7 0.1 copy.37
  15.8 0.1 select_reduce_fusion
  15.9 0.1 compare_convert_fusion
  16.0 0.1 and_select_fusion.2
  16.1 0.7 stack.2.index_ref
  16.7 1.6 %fusion.3 = bf16[128,1280]{0,1:T(8,128)(2,1)S(1)} fusion(bf16[128,936]{1,0:T(8,128)(2,1)S(1)} %bitcast.13, s32[1280]{0:T(1024)} %constant.106), kind=kOutput, calls=%fused_computation.4 | convolution fusion | flops 309268480 | bytes 572416
  18.4 0.2 copy.39
  18.6 1.1 reshape_reshape.3.table_ref
  19.7 0.0 copy-start.1
  19.7 100.5 %shard_map.128 = f32[16,2,1,256]{3,2,1,0:T(1,128)} custom-call(s32[2,7]{1,0:T(2,128)} %stack.2.index_ref, f32[8,9]{1,0:T(8,128)} %omega_ref.1, bf16[2,640,128]{2,1,0:T(8,128)(2,1)} %reshape_reshape.3.table_ref, bf16[2,2,128,1536]{3,2,1,0:T(8,128)(2,1)} %coeffs_ref.1, bf16[256,160]{1,0:T(8,128)(2,1)} %constant.90.clone.pad_ref, ...), custom_call_target="tpu_custom_call" | custom-call | flops 17213423616 | bytes 3145728 | tf_op jit(solution)/shard_map/pallas_call | solution.py:420
  120.2 0.8 copy.41
  121.0 0.1 multiply_reduce_fusion
  121.1 0.0 copy-done.1
  121.1 0.7 fusion.10
  (8 shorter events, 0.1 us)
Async XLA Ops:
  0.0 1.0 copy-start
  19.7 101.4 %copy-start.1 = (s32[2,512]{1,0:T(2,128)S(1)}, s32[2,512]{1,0:T(2,128)}, u32[]{:S(2)}) copy-start(s32[2,512]{1,0:T(2,128)} %param.19) | copy-start | bytes 12292

commit v5 on v4

--- a/solution.py
+++ b/solution.py
@@ -119,29 +119,35 @@
     lax.fori_loop(1, total, one, 0)
 
 
-def exchange_kernel(workers, parts, small_ref, small_out, smalls, s_send, s_recv):
+def exchange_kernel(workers, parts, energy_ref, pair_ref, small_out, mine, smalls, s_send, s_recv):
     worker, part = lax.axis_index("wide"), lax.axis_index("narrow")
+    owned, slots = energy_ref.shape[0], pair_ref.shape[0]
+    mine[...] = jnp.zeros(mine.shape, mine.dtype)
+    mine[:owned] = energy_ref[...].astype(jnp.float32)
+    mine[owned : owned + slots, :2] = pair_ref[...].astype(jnp.float32)
     greet(workers, parts)
-    to_all(workers, parts, small_ref, smalls, s_send, s_recv, False)
-    smalls[worker * parts + part] = small_ref[...]
-    to_all(workers, parts, small_ref, smalls, s_send, s_recv, True)
+    to_all(workers, parts, mine, smalls, s_send, s_recv, False)
+    smalls[worker * parts + part] = mine[...]
+    to_all(workers, parts, mine, smalls, s_send, s_recv, True)
     small_out[...] = smalls[...]
 
 
-def exchange(workers, parts, small):
+def exchange(workers, parts, energies, pairs):
     total = workers * parts
+    shape = (energies.shape[0] + pairs.shape[0], energies.shape[1])
     return pl.pallas_call(
         functools.partial(exchange_kernel, workers, parts),
-        in_specs=[pl.BlockSpec(memory_space=pltpu.VMEM)],
+        in_specs=[pl.BlockSpec(memory_space=pltpu.VMEM)] * 2,
         out_specs=pl.BlockSpec(memory_space=pltpu.VMEM),
-        out_shape=jax.ShapeDtypeStruct((total,) + small.shape, small.dtype),
+        out_shape=jax.ShapeDtypeStruct((total,) + shape, jnp.float32),
         scratch_shapes=[
-            pltpu.VMEM((total,) + small.shape, small.dtype),
+            pltpu.VMEM(shape, jnp.float32),
+            pltpu.VMEM((total,) + shape, jnp.float32),
             pltpu.SemaphoreType.DMA((total,)),
             pltpu.SemaphoreType.DMA((total,)),
         ],
         compiler_params=pltpu.CompilerParams(collective_id=0, has_side_effects=True),
-    )(small)
+    )(energies, pairs)
 
 
 def rate_kernel(
@@ -364,6 +370,8 @@
         stage_near(0, c)
         stage_far(0, c)
         if c == 0:
+            for pair in range(1, share):
+                stage_far(pair, 0)
             for step in range(1, parts):
                 table_arrival(step, core, t_send, t_recv).wait_recv()
                 table_arrival(step, core, tf_send, tf_recv).start()
@@ -377,7 +385,7 @@
     for pair in range(1, share):
         for c in range(CHUNKS):
             stage_near(pair, c)
-        for c in range(CHUNKS):
+        for c in range(1, CHUNKS):
             stage_far(pair, c)
     for c in range(1, CHUNKS):
         mix(0, c)
@@ -456,10 +464,8 @@
     excitons = blocks.shape[1]
 
     parts = lax.axis_size("narrow")
-    listed = jnp.pad(pairs.astype(jnp.float32).reshape(1, -1), ((0, 0), (0, columns - 2 * slots)))
-    small = exchange(workers, parts, jnp.concatenate([energies.astype(jnp.float32), listed], axis=0))
-    listed = small.reshape(workers, parts, owned + 1, columns)[:, 0, owned, : 2 * slots]
-    listed = listed.reshape(workers, slots, 2)
+    small = exchange(workers, parts, energies, pairs)
+    listed = small.reshape(workers, parts, owned + slots, columns)[:, 0, owned:, :2]
 
     before = jnp.arange(workers)[:, None] > jnp.arange(workers)[None, :]
     rank = jnp.sum(jnp.where(before, counts[None, :], 0), axis=1)[:, None] + jnp.arange(slots)[None, :]

time: 122 us -> 122 us (level)
  other arithmetic: 4.79 us -> 2.85 us
    unnamed x7 -> x8, local copies, waits for them, and re-layouts: 1.81 us -> 3.19 us
    convert_element_type x2 -> x0, other arithmetic: 1.34 us -> none  [the longest x1 0.68 us: shards(): pairs.astype(jnp.float32).reshape(1, -1)]
where the time goes in v5:
time: 122 us
  Pallas kernels  111 us (91%)
  local copies, waits for them, and re-layouts  5.99 us (5%)
  other arithmetic  2.85 us (2%)
  matrix products  1.64 us (1%)
    pallas_call x1, Pallas kernels, pair_rates(): pl.pallas_call(functools.partial(rate_kernel, workers, parts), in_specs=[...  101 us
    pallas_call x1, Pallas kernels, exchange(): pl.pallas_call(functools.partial(exchange_kernel, workers, parts), in_spe...  10.2 us
    unnamed x8, local copies, waits for them, and re-layouts  3.19 us

profile of v5, /device:TPU:0, one launch (start us, length us, event | category | flops | bytes accessed | tf_op | source)
XLA Modules:
  0.0 121.8 jit_solution(13348998782694771298)
XLA Ops:
  0.0 0.0 copy-start
  0.0 0.9 copy-done
  1.0 0.8 select_reduce_fusion.2
  1.7 0.7 add_select_fusion
  2.5 0.1 broadcast_compare_fusion
  2.5 0.1 iota_compare_fusion.1
  2.6 1.4 %copy.30.pair_ref = s32[4,2]{1,0:T(4,128)} copy(s32[4,2]{0,1:T(2,128)} %param.17) | data formatting | bytes 64 | tf_op args[4]
  4.0 10.2 %shard_map.127.small_ref = f32[16,6,128]{2,1,0:T(8,128)} custom-call(bf16[2,128]{1,0:T(2,128)(2,1)} %energy_ref.1, s32[4,2]{1,0:T(4,128)} %copy.30.pair_ref), custom_call_target="tpu_custom_call" | custom-call | tf_op jit(solution)/shard_map/pallas_call | solution.py:138
  14.2 0.7 slice_bitcast_fusion.1
  14.9 0.1 copy.32
  15.0 0.1 select_reduce_fusion
  15.1 0.1 compare_convert_fusion
  15.2 0.1 copy.36
  15.3 0.1 select_reduce_fusion.1
  15.4 0.1 and_select_fusion.2
  15.5 0.7 stack.2.index_ref
  16.2 1.6 %fusion.3 = bf16[128,1280]{0,1:T(8,128)(2,1)S(1)} fusion(bf16[128,936]{1,0:T(8,128)(2,1)S(1)} %bitcast.15, s32[1280]{0:T(1024)} %constant.104), kind=kOutput, calls=%fused_computation.4 | convolution fusion | flops 309268480 | bytes 572416
  17.8 0.2 copy.33
  18.0 1.1 reshape_reshape.3.table_ref
  19.1 0.0 copy-start.1
  19.1 101.1 %shard_map.128 = f32[16,2,1,256]{3,2,1,0:T(1,128)} custom-call(s32[2,7]{1,0:T(2,128)} %stack.2.index_ref, f32[8,9]{1,0:T(8,128)} %omega_ref.1, bf16[2,640,128]{2,1,0:T(8,128)(2,1)} %reshape_reshape.3.table_ref, bf16[2,2,128,1536]{3,2,1,0:T(8,128)(2,1)} %coeffs_ref.1, bf16[256,160]{1,0:T(8,128)(2,1)} %constant.90.clone.pad_ref, ...), custom_call_target="tpu_custom_call" | custom-call | flops 17213423616 | bytes 3145728 | tf_op jit(solution)/shard_map/pallas_call | solution.py:428
  120.2 0.8 copy.35
  121.0 0.1 multiply_reduce_fusion
  121.1 0.0 copy-done.1
  121.1 0.7 fusion.10
  (8 shorter events, 0.1 us)
Async XLA Ops:
  0.0 1.0 copy-start
  19.1 102.0 %copy-start.1 = (s32[2,512]{1,0:T(2,128)S(1)}, s32[2,512]{1,0:T(2,128)}, u32[]{:S(2)}) copy-start(s32[2,512]{1,0:T(2,128)} %param.19) | copy-start | bytes 12292
